TPU v7x, 128 devices: a whole 4x4x4 slice. The times are simulated.
128 devices in a mesh: dp: 4 (over y), expert: 32 (over x, z, core).
Axes of the slice: x: 4, y: 4, z: 4, core: 2. Of those that a mesh axis runs over, the one named last changes fastest.
Arguments:
- tokens: bfloat16 [16384, 3584], P(('dp', 'expert')), may hold values from -6 to 6
- gate_probs: float32 [16384, 8], P(('dp', 'expert')), may hold values from 0.1 to 1
- expert_ids: int32 [16384, 8], P(('dp', 'expert')), may hold values from 0 to 255, all different within a row; in each aligned block of 128 rows (0 to 127, 128 to 255, ...) at most 6 rows name the same one
- cotangent: bfloat16 [16384, 3584], P(('dp', 'expert')), may hold values from -6 to 6
- w_gate: bfloat16 [32, 3584, 2048], P('expert', None, 'dp'), may hold values from -0.09375 to 0.09375
- w_up: bfloat16 [32, 3584, 2048], P('expert', None, 'dp'), may hold values from -0.09375 to 0.09375
- w_down: bfloat16 [32, 2048, 3584], P('expert', 'dp'), may hold values from -0.125 to 0.125
Outputs:
- layer_out: bfloat16 [16384, 3584], P(('dp', 'expert'))
- grad_tokens: bfloat16 [16384, 3584], P(('dp', 'expert'))
- grad_probs: float32 [16384, 8], P(('dp', 'expert'))
- grad_gate: bfloat16 [32, 3584, 2048], P('expert', None, 'dp')
- grad_up: bfloat16 [32, 3584, 2048], P('expert', None, 'dp')
- grad_down: bfloat16 [32, 2048, 3584], P('expert', 'dp')
Inputs may be any that keep to these rules, and one draw needn't show every extreme that they name: `expert_ids`: each token names 8 distinct ids. Among the 128 tokens of one device no id is named by more than 6 of them, a bound that some block reaches. Only ids below 32 belong to the window.
All inputs are finite; a program needn't handle non-finite values.
Results may differ from a plain program's by a relative error of at most 0.012.
Values may be sent and summed in bfloat16 or wider, within the bound.
A program may use at most 192 MiB of HBM per device.

v0:
```python
import jax
import jax.numpy as jnp
from jax import lax
from jax.sharding import PartitionSpec as P


def slot_table(flat_ids, experts, capacity, sentinel):
    matches = (flat_ids[:, None] == jnp.arange(experts, dtype=jnp.int32)[None, :]).astype(jnp.int32)
    earlier = jnp.cumsum(matches, axis=0) - matches
    slot_pos = jnp.sum(earlier * matches, axis=1)
    target = jnp.where(flat_ids < experts, flat_ids * capacity + slot_pos, experts * capacity)
    flat_index = jnp.arange(flat_ids.shape[0], dtype=jnp.int32)
    blank_table = jnp.full((experts * capacity,), sentinel, jnp.int32)
    return blank_table.at[target].set(flat_index, mode="drop")


def contract_last(left, right):
    return lax.dot_general(
        left, right, (((1,), (1,)), ((), ())), preferred_element_type=jnp.float32
    )


def contract_first(left, right):
    return lax.dot_general(
        left, right, (((0,), (0,)), ((), ())), preferred_element_type=jnp.float32
    )


def on_device(tokens, gate_probs, expert_ids, cotangent, w_gate, w_up, w_down):
    tok_count, model_width = tokens.shape
    top_k = expert_ids.shape[1]
    experts = lax.axis_size("expert")
    groups = lax.axis_size("dp")
    capacity = 3 * tok_count * top_k // (16 * experts)
    flat_count = tok_count * top_k
    slots = slot_table(expert_ids.reshape(-1), experts, capacity, flat_count)
    token_of = slots // top_k
    zero_row = jnp.zeros((1, model_width), jnp.bfloat16)
    send_x = jnp.concatenate([tokens, zero_row], 0)[token_of]
    rows_dy = jnp.concatenate([cotangent, zero_row], 0)[token_of]
    prob_rows = jnp.concatenate([gate_probs.reshape(-1), jnp.zeros((1,), jnp.float32)], 0)[slots]
    send_c = (prob_rows[:, None] * rows_dy.astype(jnp.float32)).astype(jnp.bfloat16)
    fanned_x = jnp.tile(send_x, (groups, 1))
    fanned_c = jnp.tile(send_c, (groups, 1))
    rows_x, rows_c = (
        lax.all_to_all(fanned_x, ("dp", "expert"), split_axis=0, concat_axis=0, tiled=True),
        lax.all_to_all(fanned_c, ("dp", "expert"), split_axis=0, concat_axis=0, tiled=True),
    )
    gate_w = w_gate[0]
    up_w = w_up[0]
    down_w = w_down[0]
    gate_pre = jnp.dot(rows_x, gate_w, preferred_element_type=jnp.float32)
    up_pre = jnp.dot(rows_x, up_w, preferred_element_type=jnp.float32)
    sigmoid_g = jax.nn.sigmoid(gate_pre)
    activated = gate_pre * sigmoid_g
    hidden = (activated * up_pre).astype(jnp.bfloat16)
    part_out = jnp.dot(hidden, down_w, preferred_element_type=jnp.float32).astype(jnp.bfloat16)
    returned = lax.all_to_all(part_out, ("dp", "expert"), split_axis=0, concat_axis=0, tiled=True)
    out_rows = jnp.sum(
        returned.astype(jnp.float32).reshape(groups, experts * capacity, model_width), axis=0
    )
    grad_hidden = contract_last(rows_c, down_w)
    grad_upin = (grad_hidden * activated).astype(jnp.bfloat16)
    grad_gatein = (grad_hidden * up_pre * sigmoid_g * (1.0 + gate_pre * (1.0 - sigmoid_g))).astype(
        jnp.bfloat16
    )
    part_dx = (contract_last(grad_gatein, gate_w) + contract_last(grad_upin, up_w)).astype(
        jnp.bfloat16
    )
    returned_dx = lax.all_to_all(part_dx, ("dp", "expert"), split_axis=0, concat_axis=0, tiled=True)
    dx_rows = jnp.sum(
        returned_dx.astype(jnp.float32).reshape(groups, experts * capacity, model_width), axis=0
    )
    new_gate = contract_first(rows_x, grad_gatein).astype(jnp.bfloat16)[None]
    new_up = contract_first(rows_x, grad_upin).astype(jnp.bfloat16)[None]
    new_down = contract_first(hidden, rows_c).astype(jnp.bfloat16)[None]
    owner = (token_of[None, :] == jnp.arange(tok_count, dtype=jnp.int32)[:, None]).astype(
        jnp.float32
    )
    layer_out = jnp.dot(
        owner * prob_rows[None, :],
        out_rows,
        precision=lax.Precision.HIGHEST,
        preferred_element_type=jnp.float32,
    ).astype(jnp.bfloat16)
    grad_tokens = jnp.dot(
        owner, dx_rows, precision=lax.Precision.HIGHEST, preferred_element_type=jnp.float32
    ).astype(jnp.bfloat16)
    score_rows = jnp.sum(rows_dy.astype(jnp.float32) * out_rows, axis=1)
    grad_probs = (
        jnp.zeros((flat_count + 1,), jnp.float32)
        .at[slots]
        .set(score_rows)[:flat_count]
        .reshape(tok_count, top_k)
    )
    return (layer_out, grad_tokens, grad_probs, new_gate, new_up, new_down)


def solution(mesh):
    return jax.shard_map(
        on_device,
        mesh=mesh,
        in_specs=(
            P(("dp", "expert"), None),
            P(("dp", "expert"), None),
            P(("dp", "expert"), None),
            P(("dp", "expert"), None),
            P("expert", None, "dp"),
            P("expert", None, "dp"),
            P("expert", "dp", None),
        ),
        out_specs=(
            P(("dp", "expert"), None),
            P(("dp", "expert"), None),
            P(("dp", "expert"), None),
            P("expert", None, "dp"),
            P("expert", None, "dp"),
            P("expert", "dp", None),
        ),
        check_vma=False,
    )
```

profile of v0, /device:TPU:1, one launch (start us, length us, event | category | flops | bytes accessed | tf_op | source)
XLA Modules:
  0.0 477.7 jit_solution(5244566264524585080)
XLA Ops:
  3.4 9.0 %reduce-window.6 = s32[32,8,128]{2,1,0:T(8,128)S(1)} reduce-window(s32[32,8,128]{2,1,0:T(8,128)S(1)} %fusion.20, s32[]{:T(128)} %constant.18.clone.1), window={size=1x1x128 pad=0_0x0_0x127_0}, to_apply=%region_0.0 | reduce-window | flops 4161536 | bytes 262148 | tf_op jit(solution)/shard_map/reduce-window
  13.0 4.3 scatter_custom_fusion
  20.0 2.8 tile.4
  22.8 9.6 %all_to_all.28 = bf16[128,6,3584]{2,1,0:T(8,128)(2,1)} reshape(bf16[4,192,3584]{2,1,0:T(8,128)(2,1)} %tile.4) | data formatting | bytes 11010048 | tf_op jit(solution)/shard_map/all_to_all | solution.py:46
  32.4 11.9 %all-to-all-start = ((bf16[128,6,3584]{2,1,0:T(8,128)(2,1)}), bf16[128,6,3584]{2,1,0:T(8,128)(2,1)}, u32[]{:S(2)}, u32[]{:S(2)}) async-start(bf16[128,6,3584]{2,1,0:T(8,128)(2,1)} %all_to_all.28), calls=%async_computation | async-start | bytes 14680064 | tf_op jit(solution)/shard_map/all_to_all | solution.py:46
  47.8 2.8 tile.5
  50.6 9.6 %all_to_all.33 = bf16[128,6,3584]{2,1,0:T(8,128)(2,1)} reshape(bf16[4,192,3584]{2,1,0:T(8,128)(2,1)} %tile.5) | data formatting | bytes 11010048 | tf_op jit(solution)/shard_map/all_to_all | solution.py:47
  60.2 73.9 %all-to-all-done = bf16[128,6,3584]{2,1,0:T(8,128)(2,1)} async-done(((bf16[128,6,3584]{2,1,0:T(8,128)(2,1)}), bf16[128,6,3584]{2,1,0:T(8,128)(2,1)}, u32[]{:S(2)}, u32[]{:S(2)}) %all-to-all-start) | async-done | bytes 5505056 | tf_op jit(solution)/shard_map/all_to_all | solution.py:46
  134.1 7.3 %all-to-all-start.2 = ((bf16[128,6,3584]{2,1,0:T(8,128)(2,1)}), bf16[128,6,3584]{2,1,0:T(8,128)(2,1)}, u32[]{:S(2)}, u32[]{:S(2)}) async-start(bf16[128,6,3584]{2,1,0:T(8,128)(2,1)} %all_to_all.33), calls=%async_computation.2 | async-start | bytes 14680064 | tf_op jit(solution)/shard_map/all_to_all | solution.py:47
  141.4 9.7 %all_to_all.30 = bf16[768,3584]{1,0:T(8,128)(2,1)} reshape(bf16[128,6,3584]{2,1,0:T(8,128)(2,1)} %all-to-all-done) | data formatting | bytes 11010048 | tf_op jit(solution)/shard_map/all_to_all | solution.py:46
  151.1 7.9 %fusion.7 = f32[768,512]{1,0:T(8,128)} fusion(bf16[768,3584]{1,0:T(8,128)(2,1)} %all_to_all.30, bf16[1,3584,512]{2,1,0:T(8,128)(2,1)} %param.12), kind=kOutput, calls=%fused_computation.19 | convolution fusion | flops 2818572288 | bytes 10747904 | tf_op jit(solution)/shard_map/dot_general | solution.py:53
  159.0 4.1 fusion.11
  163.2 68.0 %all-to-all-done.2 = bf16[128,6,3584]{2,1,0:T(8,128)(2,1)} async-done(((bf16[128,6,3584]{2,1,0:T(8,128)(2,1)}), bf16[128,6,3584]{2,1,0:T(8,128)(2,1)}, u32[]{:S(2)}, u32[]{:S(2)}) %all-to-all-start.2) | async-done | bytes 5505056 | tf_op jit(solution)/shard_map/all_to_all | solution.py:47
  231.2 9.6 %all_to_all.35 = bf16[768,3584]{1,0:T(8,128)(2,1)} reshape(bf16[128,6,3584]{2,1,0:T(8,128)(2,1)} %all-to-all-done.2) | data formatting | bytes 11010048 | tf_op jit(solution)/shard_map/all_to_all | solution.py:47
  240.8 8.3 %multiply_convert_fusion = (bf16[768,512]{1,0:T(8,128)(2,1)S(1)}, bf16[768,512]{1,0:T(8,128)(2,1)S(1)}, bf16[768,512]{1,0:T(8,128)(2,1)S(1)}) fusion(f32[768,512]{1,0:T(8,128)} %fusion.11, f32[768,512]{1,0:T(8,128)} %fusion.7, bf16[768,3584]{1,0:T(8,128)(2,1)} %all_to_all.35, bf16[1,512,3584]{2,1,0:T(8,128)(2,1)} %param.13), kind=kOutput, calls=%fused_computation.29 | convolution fusion | flops 2824470528 | bytes 14680064 | tf_op jit(solution)/shard_map/dot_general | solution.py:18
  249.1 4.8 %convolution_convert_fusion = bf16[768,3584]{1,0:T(8,128)(2,1)} fusion(bf16[768,512]{1,0:T(8,128)(2,1)S(1)} %get-tuple-element.16, bf16[1,512,3584]{2,1,0:T(8,128)(2,1)S(1)} %copy-done.4), kind=kOutput, calls=%fused_computation.6 | convolution fusion | flops 2821324800 | bytes 9961472 | tf_op jit(solution)/shard_map/dot_general | solution.py:57
  253.9 9.6 %all_to_all.31 = bf16[128,6,3584]{2,1,0:T(8,128)(2,1)} reshape(bf16[768,3584]{1,0:T(8,128)(2,1)} %convolution_convert_fusion) | data formatting | bytes 11010048 | tf_op jit(solution)/shard_map/all_to_all | solution.py:58
  263.5 8.7 %all-to-all-start.1 = ((bf16[128,6,3584]{2,1,0:T(8,128)(2,1)}), bf16[128,6,3584]{2,1,0:T(8,128)(2,1)}, u32[]{:S(2)}, u32[]{:S(2)}) async-start(bf16[128,6,3584]{2,1,0:T(8,128)(2,1)} %all_to_all.31), calls=%async_computation.1 | async-start | bytes 14680064 | tf_op jit(solution)/shard_map/all_to_all | solution.py:58
  272.3 5.2 %fusion.9 = f32[768,3584]{1,0:T(8,128)S(1)} fusion(bf16[768,512]{1,0:T(8,128)(2,1)S(1)} %get-tuple-element.15, bf16[1,3584,512]{2,1,0:T(8,128)(2,1)} %param.11), kind=kOutput, calls=%fused_computation.21 | convolution fusion | flops 2818572288 | bytes 15466496 | tf_op jit(solution)/shard_map/dot_general | solution.py:18
  277.5 4.9 %add_convert_fusion = bf16[768,3584]{1,0:T(8,128)(2,1)} fusion(f32[768,3584]{1,0:T(8,128)S(1)} %fusion.9, bf16[768,512]{1,0:T(8,128)(2,1)S(1)} %get-tuple-element.14, bf16[1,3584,512]{2,1,0:T(8,128)(2,1)S(1)} %copy-done.6), kind=kOutput, calls=%fused_computation.5 | convolution fusion | flops 2824077312 | bytes 20971520 | tf_op jit(solution)/shard_map/dot_general | solution.py:18
  282.4 9.6 %all_to_all.36 = bf16[128,6,3584]{2,1,0:T(8,128)(2,1)} reshape(bf16[768,3584]{1,0:T(8,128)(2,1)} %add_convert_fusion) | data formatting | bytes 11010048 | tf_op jit(solution)/shard_map/all_to_all | solution.py:70
  292.0 70.1 %all-to-all-done.1 = bf16[128,6,3584]{2,1,0:T(8,128)(2,1)} async-done(((bf16[128,6,3584]{2,1,0:T(8,128)(2,1)}), bf16[128,6,3584]{2,1,0:T(8,128)(2,1)}, u32[]{:S(2)}, u32[]{:S(2)}) %all-to-all-start.1) | async-done | bytes 5505056 | tf_op jit(solution)/shard_map/all_to_all | solution.py:58
  362.0 7.3 %all-to-all-start.3 = ((bf16[128,6,3584]{2,1,0:T(8,128)(2,1)}), bf16[128,6,3584]{2,1,0:T(8,128)(2,1)}, u32[]{:S(2)}, u32[]{:S(2)}) async-start(bf16[128,6,3584]{2,1,0:T(8,128)(2,1)} %all_to_all.36), calls=%async_computation.3 | async-start | bytes 14680064 | tf_op jit(solution)/shard_map/all_to_all | solution.py:70
  369.3 7.2 %fusion.2 = bf16[1,512,3584]{2,1,0:T(8,128)(2,1)} fusion(bf16[768,512]{1,0:T(8,128)(2,1)S(1)} %get-tuple-element.16, bf16[768,3584]{1,0:T(8,128)(2,1)} %all_to_all.35), kind=kOutput, calls=%fused_computation.12 | convolution fusion | flops 2820407296 | bytes 9961472 | tf_op jit(solution)/shard_map/dot_general | solution.py:24
  376.6 7.2 %fusion.1 = bf16[1,3584,512]{2,1,0:T(8,128)(2,1)} fusion(bf16[768,3584]{1,0:T(8,128)(2,1)} %all_to_all.30, bf16[768,512]{1,0:T(8,128)(2,1)S(1)} %get-tuple-element.14), kind=kOutput, calls=%fused_computation.11 | convolution fusion | flops 2820407296 | bytes 9961472 | tf_op jit(solution)/shard_map/dot_general | solution.py:24
  383.8 4.6 fusion
  388.3 10.9 %reshape.124 = f32[4,192,3584]{2,1,0:T(8,128)} reshape(bf16[128,6,3584]{2,1,0:T(8,128)(2,1)} %all-to-all-done.1) | data formatting | bytes 16515072 | tf_op jit(solution)/shard_map/convert_element_type | solution.py:60
  399.2 5.4 %reduce_sum.40 = f32[192,3584]{1,0:T(8,128)S(1)} reduce(f32[4,192,3584]{2,1,0:T(8,128)} %reshape.124, f32[]{:T(128)} %constant.42.clone.1), dimensions={0}, to_apply=%region_4.5 | reduce | flops 2064384 | bytes 13762564 | tf_op jit(solution)/shard_map/reduce_sum | solution.py:59
  408.6 2.7 convolution_convert_fusion.5
  411.2 47.9 %all-to-all-done.3 = bf16[128,6,3584]{2,1,0:T(8,128)(2,1)} async-done(((bf16[128,6,3584]{2,1,0:T(8,128)(2,1)}), bf16[128,6,3584]{2,1,0:T(8,128)(2,1)}, u32[]{:S(2)}, u32[]{:S(2)}) %all-to-all-start.3) | async-done | bytes 5505056 | tf_op jit(solution)/shard_map/all_to_all | solution.py:70
  459.1 10.9 %reshape.125 = f32[4,192,3584]{2,1,0:T(8,128)} reshape(bf16[128,6,3584]{2,1,0:T(8,128)(2,1)} %all-to-all-done.3) | data formatting | bytes 16515072 | tf_op jit(solution)/shard_map/convert_element_type | solution.py:72
  470.0 5.4 %reduce_sum.41 = f32[192,3584]{1,0:T(8,128)S(1)} reduce(f32[4,192,3584]{2,1,0:T(8,128)} %reshape.125, f32[]{:T(128)} %constant.42.clone.1), dimensions={0}, to_apply=%region_5.6 | reduce | flops 2064384 | bytes 13762564 | tf_op jit(solution)/shard_map/reduce_sum | solution.py:71
  (55 shorter events, 15.6 us)
Async XLA Ops:
  32.4 11.9 %copy-start.3 = (f32[128,8]{0,1:T(8,128)S(1)}, f32[128,8]{0,1:T(8,128)}, u32[]{:S(2)}) copy-start(f32[128,8]{0,1:T(8,128)} %param.8) | copy-start | bytes 12292
  32.4 12.1 %copy-start.2 = (bf16[128,3584]{1,0:T(8,128)(2,1)S(1)}, bf16[128,3584]{1,0:T(8,128)(2,1)}, u32[]{:S(2)}) copy-start(bf16[128,3584]{1,0:T(8,128)(2,1)} %param.10) | copy-start | bytes 2752516
  32.4 101.7 %all-to-all-start = ((bf16[128,6,3584]{2,1,0:T(8,128)(2,1)}), bf16[128,6,3584]{2,1,0:T(8,128)(2,1)}, u32[]{:S(2)}, u32[]{:S(2)}) async-start(bf16[128,6,3584]{2,1,0:T(8,128)(2,1)} %all_to_all.28), calls=%async_computation | async-start | bytes 14680064 | tf_op jit(solution)/shard_map/all_to_all | solution.py:46
  46.0 4.6 copy-start
  134.1 97.1 %all-to-all-start.2 = ((bf16[128,6,3584]{2,1,0:T(8,128)(2,1)}), bf16[128,6,3584]{2,1,0:T(8,128)(2,1)}, u32[]{:S(2)}, u32[]{:S(2)}) async-start(bf16[128,6,3584]{2,1,0:T(8,128)(2,1)} %all_to_all.33), calls=%async_computation.2 | async-start | bytes 14680064 | tf_op jit(solution)/shard_map/all_to_all | solution.py:47
  151.1 7.9 %copy-start.1 = (bf16[768,3584]{1,0:T(8,128)(2,1)S(1)}, bf16[768,3584]{1,0:T(8,128)(2,1)}, u32[]{:S(2)}) copy-start(bf16[768,3584]{1,0:T(8,128)(2,1)} %all_to_all.30) | copy-start | bytes 16515076
  151.1 8.0 %copy-start.5 = (bf16[1,3584,512]{2,1,0:T(8,128)(2,1)S(1)}, bf16[1,3584,512]{2,1,0:T(8,128)(2,1)}, u32[]{:S(2)}) copy-start(bf16[1,3584,512]{2,1,0:T(8,128)(2,1)} %param.11) | copy-start | bytes 11010052
  240.8 8.3 %copy-start.4 = (bf16[1,512,3584]{2,1,0:T(8,128)(2,1)S(1)}, bf16[1,512,3584]{2,1,0:T(8,128)(2,1)}, u32[]{:S(2)}) copy-start(bf16[1,512,3584]{2,1,0:T(8,128)(2,1)} %param.13) | copy-start | bytes 11010052
  263.5 98.5 %all-to-all-start.1 = ((bf16[128,6,3584]{2,1,0:T(8,128)(2,1)}), bf16[128,6,3584]{2,1,0:T(8,128)(2,1)}, u32[]{:S(2)}, u32[]{:S(2)}) async-start(bf16[128,6,3584]{2,1,0:T(8,128)(2,1)} %all_to_all.31), calls=%async_computation.1 | async-start | bytes 14680064 | tf_op jit(solution)/shard_map/all_to_all | solution.py:58
  272.2 5.3 %copy-start.6 = (bf16[1,3584,512]{2,1,0:T(8,128)(2,1)S(1)}, bf16[1,3584,512]{2,1,0:T(8,128)(2,1)}, u32[]{:S(2)}) copy-start(bf16[1,3584,512]{2,1,0:T(8,128)(2,1)} %param.12) | copy-start | bytes 11010052
  362.0 97.1 %all-to-all-start.3 = ((bf16[128,6,3584]{2,1,0:T(8,128)(2,1)}), bf16[128,6,3584]{2,1,0:T(8,128)(2,1)}, u32[]{:S(2)}, u32[]{:S(2)}) async-start(bf16[128,6,3584]{2,1,0:T(8,128)(2,1)} %all_to_all.36), calls=%async_computation.3 | async-start | bytes 14680064 | tf_op jit(solution)/shard_map/all_to_all | solution.py:70
  369.3 14.4 %slice-start = ((s8[5505024]{0:T(1024)(128)(4,1)}), s8[4194304]{0:T(1024)(128)(4,1)S(1)}, s32[]{:S(2)}) async-start(s8[5505024]{0:T(1024)(128)(4,1)} %bitcast.59), calls=%async_computation.4 | async-start | bytes 8388608
  376.6 7.2 %slice-start.1 = ((s8[5505024]{0:T(1024)(128)(4,1)}), s8[1310720]{0:T(1024)(128)(4,1)S(1)}, s32[]{:S(2)}) async-start(s8[5505024]{0:T(1024)(128)(4,1)} %bitcast.59), calls=%async_computation.5 | async-start | bytes 2621440
where the time goes:
time: 480 us; the launch traced here: 478 us
  waiting for transfers between devices  260 us (54%)
  local copies, waits for them, and re-layouts  99 us (21%)
  matrix products  59.2 us (12%)
  starting transfers between devices  35.3 us (7%)
  other arithmetic  23.5 us (5%)
    all_to_all x1, waiting for transfers between devices, on_device(): lax.all_to_all(fanned_x, ('dp', 'expert'), split_axis=0, concat_axis=0, t...  73.9 us
    all_to_all x1, waiting for transfers between devices, on_device(): lax.all_to_all(part_out, ('dp', 'expert'), split_axis=0, concat_axis=0, t...  70.1 us
    all_to_all x1, waiting for transfers between devices, on_device(): lax.all_to_all(fanned_c, ('dp', 'expert'), split_axis=0, concat_axis=0, t...  68 us
    all_to_all x1, waiting for transfers between devices, on_device(): lax.all_to_all(part_dx, ('dp', 'expert'), split_axis=0, concat_axis=0, ti...  47.9 us
    all_to_all x2, local copies, waits for them, and re-layouts, on_device(): lax.all_to_all(fanned_x, ('dp', 'expert'), split_axis=0, concat_axis=0, t...  19.3 us
    all_to_all x2, local copies, waits for them, and re-layouts, on_device(): lax.all_to_all(fanned_c, ('dp', 'expert'), split_axis=0, concat_axis=0, t...  19.2 us
    dot_general x3, matrix products, contract_first(): lax.dot_general(left, right, (((0,), (0,)), ((), ())), preferred_element_...  19 us
    dot_general x3, matrix products, contract_last(): lax.dot_general(left, right, (((1,), (1,)), ((), ())), preferred_element_...  18.4 us
  transfers between devices with their start and end apart: 4, of which 4 were waited for; matrix products, arithmetic and copies ran while one was open for 15% of the time, Pallas kernels for 0%

commit v1 on v0

v1 whole, which is shorter than its diff:
```python
import jax
import jax.numpy as jnp
from jax import lax
from jax.experimental import pallas as pl
from jax.experimental.pallas import tpu as pltpu
from jax.sharding import PartitionSpec as P

MESH = pl.DeviceIdType.MESH
F32 = jnp.float32
BF16 = jnp.bfloat16

D = 3584
FF = 512
TOK = 128
TOP = 8
CAP = 6
NE = 32
NY = 4
NC = 7
CW = D // NC
BLK = 16
PR = NE * BLK
SR = NE * CAP
ROWS = NY * SR
A0 = NC * PR
R0 = 9 * PR


def mo(v, m):
    return pl.multiple_of(v, m)


def nn(a, b):
    return lax.dot_general(a, b, (((1,), (0,)), ((), ())), preferred_element_type=F32)


def nt(a, b):
    return lax.dot_general(a, b, (((1,), (1,)), ((), ())), preferred_element_type=F32)


def tn(a, b):
    return lax.dot_general(a, b, (((0,), (0,)), ((), ())), preferred_element_type=F32)


def kernel(
    tok, probs, ids, cot, wg_hbm, wu_hbm, wd_hbm,
    lo_out, gt_out, gp_out, gg_hbm, gu_hbm, gd_hbm,
    sa, gath, wg, wu, wd, accg, accu, acch, hid, ggi, gui,
    relay, vrec, back, stg, gsel, psel, wout, pack, zacc,
    wsem, asend, arecv, ysend, yrecv, rsend, rrecv, bsend, brecv, gsem,
):
    y = lax.axis_index("dp")
    e = lax.axis_index("expert")
    right, left, across = lax.rem(y + 1, NY), lax.rem(y + 3, NY), lax.rem(y + 2, NY)
    ex, ez, ec = e // 8, lax.rem(e // 2, 4), lax.rem(e, 2)

    def peer(j):
        jx, jz, jc = j // 8, lax.rem(j // 2, 4), lax.rem(j, 2)
        return lax.rem(ex + jx, 4) * 8 + lax.rem(ez + jz, 4) * 2 + lax.rem(ec + jc, 2)

    barrier = pltpu.get_barrier_semaphore()

    def greet(j, carry):
        pl.semaphore_signal(barrier, inc=1, device_id=(y, peer(j)), device_id_type=MESH)
        return carry

    lax.fori_loop(1, NE, greet, 0)
    for side in (right, left):
        pl.semaphore_signal(barrier, inc=1, device_id=(side, e), device_id_type=MESH)

    def weight_copies(n):
        cols = pl.ds(mo(n * CW, CW), CW)
        return (
            pltpu.make_async_copy(wg_hbm.at[cols], wg.at[n], wsem.at[0, n]),
            pltpu.make_async_copy(wu_hbm.at[cols], wu.at[n], wsem.at[1, n]),
            pltpu.make_async_copy(wd_hbm.at[:, cols], wd.at[n], wsem.at[2, n]),
        )

    def start_weights(n, carry):
        for c in weight_copies(n):
            c.start()
        return carry

    lax.fori_loop(0, NC, start_weights, 0)

    lane = lax.broadcasted_iota(jnp.int32, (TOK, TOK), 1)
    sub = lax.broadcasted_iota(jnp.int32, (TOK, TOK), 0)
    named = jnp.zeros((TOK, TOK), F32)
    weight = jnp.zeros((TOK, TOK), F32)
    for k in range(TOP):
        hit = ids[:, k : k + 1] == lane
        named = named + jnp.where(hit, 1.0, 0.0)
        weight = weight + jnp.where(hit, probs[:, k : k + 1], 0.0)
    before = jnp.where(lane < sub, 1.0, 0.0).astype(BF16)
    rank = nn(before, named.astype(BF16))
    code = jnp.where(named > 0.5, rank, 255.0).T[:NE]
    code = jnp.broadcast_to(code[:, None, :], (NE, BLK, TOK)).reshape(PR, TOK)
    weight = jnp.broadcast_to(weight.T[:NE][:, None, :], (NE, BLK, TOK)).reshape(PR, TOK)
    place = lax.rem(lax.broadcasted_iota(jnp.int32, (PR, TOK), 0), BLK)
    slot = place.astype(F32)
    sel_x = jnp.where((place < CAP) & (code == slot), 1.0, 0.0)
    sel_c = jnp.where((place >= CAP) & (place < 2 * CAP) & (code == slot - CAP), 1.0, 0.0)
    gsel[0] = sel_x.astype(BF16)
    gsel[1] = sel_c.astype(BF16)
    psel[...] = jnp.broadcast_to(jnp.sum(sel_c * weight, axis=1, keepdims=True), (PR, TOK))
    by_token = (sel_x * weight).T
    high = by_token.astype(BF16)
    wout[0] = high
    wout[1] = (by_token - high.astype(F32)).astype(BF16)
    wout[2] = sel_c.T.astype(BF16)
    wout[3] = sel_x.T.astype(BF16)
    r_i = lax.broadcasted_iota(jnp.int32, (2 * SR, PR), 0)
    q_i = lax.broadcasted_iota(jnp.int32, (2 * SR, PR), 1)
    kind = jnp.where(r_i >= SR, 1, 0)
    r_i = r_i - kind * SR
    src = r_i // CAP
    pack[...] = jnp.where(q_i == src * BLK + kind * CAP + (r_i - src * CAP), 1.0, 0.0).astype(BF16)
    zacc[...] = jnp.zeros((TOK, PR), F32)

    pl.semaphore_wait(barrier, NE + 1)

    def plane_out(n):
        cols = pl.ds(mo(n * CW, CW), CW)
        rows = nn(gsel[0], tok[:, cols])
        crow = nn(gsel[1], cot[:, cols])
        p = psel[:, 0:1]
        base = mo(n * PR, PR)
        sa[pl.ds(base, PR), :] = (rows + p * crow).astype(BF16)
        sa[pl.ds(mo(A0 + n * PR + e * BLK, BLK), BLK), :] = sa[pl.ds(mo(base + e * BLK, BLK), BLK), :]

        def send(j, carry):
            t = peer(j)
            pltpu.make_async_remote_copy(
                sa.at[pl.ds(mo(n * PR + t * BLK, BLK), BLK)],
                sa.at[pl.ds(mo(A0 + n * PR + e * BLK, BLK), BLK)],
                asend.at[n], arecv.at[n], device_id=(y, t), device_id_type=MESH,
            ).start()
            return carry

        lax.fori_loop(1, NE, send, 0)

    def wait_plane(sem):
        blocks = sa.at[pl.ds(0, PR - BLK)]
        pltpu.make_async_copy(blocks, blocks, sem).wait()

    def own_copy(n, kind, d):
        ref = gath.at[n, kind, y]
        return pltpu.make_async_remote_copy(
            ref, ref, ysend.at[d, kind, n], yrecv.at[d, kind, n],
            device_id=((right, left)[d], e), device_id_type=MESH,
        )

    def pass_copy(n, d):
        ref = gath.at[n, d, (left, right)[d]]
        return pltpu.make_async_remote_copy(
            ref, ref, ysend.at[d, 2, n], yrecv.at[d, 2, n],
            device_id=((right, left)[d], e), device_id_type=MESH,
        )

    plane_out(0)
    plane_out(1)
    accg[...] = jnp.zeros((ROWS, FF), F32)
    accu[...] = jnp.zeros((ROWS, FF), F32)
    acch[...] = jnp.zeros((ROWS, FF), F32)

    def gather_step(i, carry):
        @pl.when(i + 2 < NC)
        def _():
            plane_out(i + 2)

        @pl.when(i < NC)
        def _():
            wait_plane(arecv.at[i])
            both = nn(pack[...], sa[pl.ds(mo(A0 + i * PR, PR), PR), :]).astype(BF16)
            gath[i, 0, y] = both[:SR]
            gath[i, 1, y] = both[SR:]
            for kind in range(2):
                for d in range(2):
                    own_copy(i, kind, d).start()

        @pl.when((i >= 1) & (i <= NC))
        def _():
            n = i - 1
            for d in range(2):
                own_copy(n, d, d).wait_recv()
                pass_copy(n, d).start()
            for d in range(2):
                own_copy(n, 1 - d, d).wait_recv()

        @pl.when(i >= 2)
        def _():
            n = i - 2
            for d in range(2):
                pass_copy(n, d).wait_recv()
            for c in weight_copies(n):
                c.wait()

            def half(h, carry2):
                rows = pl.ds(mo(h * 2 * SR, 2 * SR), 2 * SR)
                xr = gath[n, 0, pl.ds(2 * h, 2)].reshape(2 * SR, CW)
                cr = gath[n, 1, pl.ds(2 * h, 2)].reshape(2 * SR, CW)
                accg[rows, :] += nn(xr, wg[n])
                accu[rows, :] += nn(xr, wu[n])
                acch[rows, :] += nt(cr, wd[n])
                return carry2

            lax.fori_loop(0, 2, half, 0)

        return carry

    lax.fori_loop(0, NC + 2, gather_step, 0)

    def activate(i, carry):
        rows = pl.ds(mo(i * 32, 32), 32)
        g, u, h = accg[rows, :], accu[rows, :], acch[rows, :]
        s = jax.nn.sigmoid(g)
        act = g * s
        hid[rows, :] = (act * u).astype(BF16)
        gui[rows, :] = (h * act).astype(BF16)
        ggi[rows, :] = (h * u * s * (1.0 + g * (1.0 - s))).astype(BF16)
        return carry

    lax.fori_loop(0, ROWS // 32, activate, 0)

    def drain(n, carry):
        wait_plane(asend.at[n])
        for d in range(2):
            for kind in range(2):
                own_copy(n, kind, d).wait_send()
            pass_copy(n, d).wait_send()
        return carry

    lax.fori_loop(0, NC, drain, 0)

    def part(m, kind, b):
        return pl.ds(mo(lax.rem(m, 3) * (2 * ROWS) + kind * ROWS + b * SR, SR), SR)

    def relay_copy(m, d):
        return pltpu.make_async_remote_copy(
            sa.at[part(m, d, across)], relay.at[m, d], rsend.at[d, 2, m], rrecv.at[d, 2, m],
            device_id=((right, left)[d], e), device_id_type=MESH,
        )

    def final_copy(m, kind, d):
        return pltpu.make_async_remote_copy(
            sa.at[part(m, kind, (right, left)[d])], vrec.at[m, d, kind],
            rsend.at[d, kind, m], rrecv.at[d, kind, m],
            device_id=((right, left)[d], e), device_id_type=MESH,
        )

    def sent(m):
        for d in range(2):
            relay_copy(m, d).wait_send()
            for kind in range(2):
                final_copy(m, kind, d).wait_send()

    def grad_copies(m):
        cols = pl.ds(mo(m * CW, CW), CW)
        b = lax.rem(m, 2)
        return (
            pltpu.make_async_copy(stg.at[b, 0], gg_hbm.at[cols], gsem.at[0, m]),
            pltpu.make_async_copy(stg.at[b, 1], gu_hbm.at[cols], gsem.at[1, m]),
            pltpu.make_async_copy(stg.at[b, 2], gd_hbm.at[:, cols], gsem.at[2, m]),
        )

    def back_slot(m):
        return R0 + lax.rem(m, 3) * PR

    def scatter_step(i, carry):
        @pl.when(i < NC)
        def _():
            m = i

            @pl.when(m >= 3)
            def _():
                sent(m - 3)

            def half(h, carry2):
                rows = pl.ds(mo(h * 2 * SR, 2 * SR), 2 * SR)
                base = lax.rem(m, 3) * (2 * ROWS) + h * 2 * SR
                sa[pl.ds(mo(base, SR), 2 * SR), :] = nn(hid[rows, :], wd[m]).astype(BF16)
                dx = nt(ggi[rows, :], wg[m]) + nt(gui[rows, :], wu[m])
                sa[pl.ds(mo(base + ROWS, SR), 2 * SR), :] = dx.astype(BF16)
                return carry2

            lax.fori_loop(0, 2, half, 0)
            for d in range(2):
                relay_copy(m, d).start()
            for d in range(2):
                final_copy(m, 1 - d, d).start()

        @pl.when((i >= 1) & (i <= NC))
        def _():
            m = i - 1
            for d in range(2):
                relay_copy(m, d).wait_recv()
                rows = part(m, d, (right, left)[d])
                sa[rows, :] = (sa[rows, :].astype(F32) + relay[m, d].astype(F32)).astype(BF16)
                final_copy(m, d, d).start()

        @pl.when((i >= 2) & (i <= NC + 1))
        def _():
            m = i - 2
            for d in range(2):
                for kind in range(2):
                    final_copy(m, kind, d).wait_recv()

            @pl.when(m >= 3)
            def _():
                wait_plane(bsend.at[m - 3])

            total = []
            for kind in range(2):
                own = sa[part(m, kind, y), :].astype(F32)
                total.append((own + vrec[m, 0, kind].astype(F32) + vrec[m, 1, kind].astype(F32)).astype(BF16))
            base = back_slot(m)
            spread = tn(pack[:SR, :], total[0]) + tn(pack[SR:, :], total[1])
            sa[pl.ds(mo(base, PR), PR), :] = spread.astype(BF16)
            back[m, pl.ds(mo(e * BLK, BLK), BLK), :] = sa[pl.ds(mo(base + e * BLK, BLK), BLK), :]

            def send(j, carry2):
                t = peer(j)
                pltpu.make_async_remote_copy(
                    sa.at[pl.ds(mo(base + t * BLK, BLK), BLK)],
                    back.at[m, pl.ds(mo(e * BLK, BLK), BLK)],
                    bsend.at[m], brecv.at[m], device_id=(y, t), device_id_type=MESH,
                ).start()
                return carry2

            lax.fori_loop(1, NE, send, 0)

        @pl.when(i < NC)
        def _():
            m = i

            @pl.when(m >= 2)
            def _():
                for c in grad_copies(m - 2):
                    c.wait()

            b = lax.rem(m, 2)
            xr = gath[m, 0].reshape(ROWS, CW)
            stg[b, 0] = tn(xr, ggi[...]).astype(BF16)
            stg[b, 1] = tn(xr, gui[...]).astype(BF16)
            stg[b, 2] = tn(hid[...], gath[m, 1].reshape(ROWS, CW)).astype(BF16)
            for c in grad_copies(m):
                c.start()

        @pl.when(i >= 3)
        def _():
            m = i - 3
            wait_plane(brecv.at[m])
            cols = pl.ds(mo(m * CW, CW), CW)
            blocks = back[m]
            lo_out[:, cols] = (nn(wout[0], blocks) + nn(wout[1], blocks)).astype(BF16)
            gt_out[:, cols] = nn(wout[2], blocks).astype(BF16)
            zacc[...] += nt(cot[:, cols], blocks)

        return carry

    lax.fori_loop(0, NC + 3, scatter_step, 0)

    z = zacc[...] * wout[3].astype(F32)
    owner = lax.broadcasted_iota(jnp.int32, (TOK, PR), 1) // BLK
    for k in range(TOP):
        gp_out[:, k : k + 1] = jnp.sum(jnp.where(owner == ids[:, k : k + 1], z, 0.0), axis=1, keepdims=True)

    for m in range(NC - 3, NC):
        sent(m)
        wait_plane(bsend.at[m])
    for m in range(NC - 2, NC):
        for c in grad_copies(m):
            c.wait()


def on_device(tokens, gate_probs, expert_ids, cotangent, w_gate, w_up, w_down):
    vm = pl.BlockSpec(memory_space=pltpu.VMEM)
    hbm = pl.BlockSpec(memory_space=pl.ANY)
    dma = pltpu.SemaphoreType.DMA
    flops = 9 * 2 * ROWS * D * FF
    lo, gt, gp, gg, gu, gd = pl.pallas_call(
        kernel,
        out_shape=(
            jax.ShapeDtypeStruct((TOK, D), BF16),
            jax.ShapeDtypeStruct((TOK, D), BF16),
            jax.ShapeDtypeStruct((TOK, TOP), F32),
            jax.ShapeDtypeStruct((D, FF), BF16),
            jax.ShapeDtypeStruct((D, FF), BF16),
            jax.ShapeDtypeStruct((FF, D), BF16),
        ),
        in_specs=[vm, vm, vm, vm, hbm, hbm, hbm],
        out_specs=(vm, vm, vm, hbm, hbm, hbm),
        scratch_shapes=[
            pltpu.VMEM((2 * NC * PR, CW), BF16),
            pltpu.VMEM((NC, 2, NY, SR, CW), BF16),
            pltpu.VMEM((NC, CW, FF), BF16),
            pltpu.VMEM((NC, CW, FF), BF16),
            pltpu.VMEM((NC, FF, CW), BF16),
            pltpu.VMEM((ROWS, FF), F32),
            pltpu.VMEM((ROWS, FF), F32),
            pltpu.VMEM((ROWS, FF), F32),
            pltpu.VMEM((ROWS, FF), BF16),
            pltpu.VMEM((ROWS, FF), BF16),
            pltpu.VMEM((ROWS, FF), BF16),
            pltpu.VMEM((NC, 2, SR, CW), BF16),
            pltpu.VMEM((NC, 2, 2, SR, CW), BF16),
            pltpu.VMEM((NC, PR, CW), BF16),
            pltpu.VMEM((2, 3, CW, FF), BF16),
            pltpu.VMEM((2, PR, TOK), BF16),
            pltpu.VMEM((PR, TOK), F32),
            pltpu.VMEM((4, TOK, PR), BF16),
            pltpu.VMEM((2 * SR, PR), BF16),
            pltpu.VMEM((TOK, PR), F32),
            dma((3, NC)), dma((NC,)), dma((NC,)),
            dma((2, 3, NC)), dma((2, 3, NC)), dma((2, 3, NC)), dma((2, 3, NC)),
            dma((NC,)), dma((NC,)), dma((3, NC)),
        ],
        compiler_params=pltpu.CompilerParams(
            collective_id=0, has_side_effects=True, vmem_limit_bytes=62 * 2**20
        ),
        cost_estimate=pl.CostEstimate(flops=flops, bytes_accessed=26 * 2**20, transcendentals=ROWS * FF),
    )(tokens, gate_probs, expert_ids, cotangent, w_gate[0], w_up[0], w_down[0])
    return lo, gt, gp, gg[None], gu[None], gd[None]


def solution(mesh):
    rows = P(("dp", "expert"), None)
    wide = P("expert", None, "dp")
    tall = P("expert", "dp", None)
    return jax.shard_map(
        on_device,
        mesh=mesh,
        in_specs=(rows, rows, rows, rows, wide, wide, tall),
        out_specs=(rows, rows, rows, wide, wide, tall),
        check_vma=False,
    )
```

time: 480 us -> 241 us (0.50)
  waiting for transfers between devices: 260 us -> 0 us
  Pallas kernels: 0 us -> 222 us
  local copies, waits for them, and re-layouts: 99 us -> 18.1 us
  matrix products: 59.2 us -> 0 us
  starting transfers between devices: 35.3 us -> 0 us
  other arithmetic: 23.5 us -> 0 us
    all_to_all x4 -> x0, waiting for transfers between devices: 260 us -> none  [the longest x1 73.9 us: on_device(): lax.all_to_all(fanned_x, ('dp', 'expert'), split_axis=0, concat_axis=0, t...]
    pallas_call x0 -> x1, Pallas kernels: none -> 222 us  [on_device(): pl.pallas_call(kernel, out_shape=(jax.ShapeDtypeStruct((TOK, D), BF16), j...]
    dot_general x11 -> x0, matrix products: 59.2 us -> none  [the longest x3 19 us: contract_first(): lax.dot_general(left, right, (((0,), (0,)), ((), ())), preferred_element_...]
    all_to_all x6 -> x0, local copies, waits for them, and re-layouts: 57.6 us -> none  [the longest x2 19.3 us: on_device(): lax.all_to_all(fanned_x, ('dp', 'expert'), split_axis=0, concat_axis=0, t...]
    all_to_all x4 -> x0, starting transfers between devices: 35.3 us -> none  [the longest x1 11.9 us: on_device(): lax.all_to_all(fanned_x, ('dp', 'expert'), split_axis=0, concat_axis=0, t...]
    convert_element_type x2 -> x0, local copies, waits for them, and re-layouts: 21.8 us -> none  [the longest x1 10.9 us: on_device(): returned_dx.astype(jnp.float32)]
    unnamed x21 -> x12, local copies, waits for them, and re-layouts: 1.59 us -> 18.1 us
    reduce_sum x4 -> x0, other arithmetic: 12.6 us -> none  [the longest x1 5.41 us: on_device(): jnp.sum(returned.astype(jnp.float32).reshape(groups, experts * capacity,...]
  transfers between devices with their start and end apart: 4 -> 0, of which waited for: 4 -> 0; matrix products, arithmetic and copies ran while one was open for 15% -> 0% of each run, Pallas kernels for 0% -> 0%
where the time goes in v1:
time: 241 us; the launch traced here: 240 us
  Pallas kernels  222 us (92%)
  local copies, waits for them, and re-layouts  18.1 us (8%)
    pallas_call x1, Pallas kernels, on_device(): pl.pallas_call(kernel, out_shape=(jax.ShapeDtypeStruct((TOK, D), BF16), j...  222 us
    unnamed x12, local copies, waits for them, and re-layouts  18.1 us

profile of v1, /device:TPU:1, one launch (start us, length us, event | category | flops | bytes accessed | tf_op | source)
XLA Modules:
  0.0 240.4 jit_solution(4617056868352776597)
XLA Ops:
  0.6 1.4 copy.13.probs
  2.0 1.4 copy.14.ids
  3.5 221.7 %shard_map.118 = (bf16[128,3584]{1,0:T(8,128)(2,1)}, bf16[128,3584]{1,0:T(8,128)(2,1)}, f32[128,8]{1,0:T(8,128)}, bf16[3584,512]{1,0:T(8,128)(2,1)}, bf16[3584,5...) custom-call(bf16[128,3584]{1,0:T(8,128)(2,1)} %tok.1, f32[128,8]{1,0:T(8,128)} %copy.13.probs, s32[128,8]{1,0:T(8,128)} %copy.14.ids, ...), custom_call_target="tpu_custom_call" | custom-call | flops 25367150592 | bytes 27262976 | tf_op jit(solution)/shard_map/pallas_call | solution.py:381
  225.1 1.5 copy.15
  226.6 2.2 copy.21
  228.8 2.2 copy.22
  231.0 0.0 copy-start.1
  231.0 4.3 %copy.23 = bf16[1,3584,512]{2,1,0:T(8,128)(2,1)} copy(bf16[1,3584,512]{2,1,0:T(8,128)(2,1)} %bitcast.8) | data formatting | bytes 7340032
  235.2 0.0 copy-done.1
  235.2 0.0 copy-start
  235.2 1.9 copy.24
  237.1 1.5 copy-done
  238.6 1.8 copy.25
Async XLA Ops:
  231.0 4.3 %copy-start.1 = (bf16[3584,512]{1,0:T(8,128)(2,1)S(1)}, bf16[3584,512]{1,0:T(8,128)(2,1)}, u32[]{:S(2)}) copy-start(bf16[3584,512]{1,0:T(8,128)(2,1)} %get-tuple-element.16) | copy-start | bytes 11010052
  235.2 3.4 %copy-start = (bf16[512,3584]{1,0:T(8,128)(2,1)S(1)}, bf16[512,3584]{1,0:T(8,128)(2,1)}, u32[]{:S(2)}) copy-start(bf16[512,3584]{1,0:T(8,128)(2,1)} %get-tuple-element.17) | copy-start | bytes 11010052

commit v2 on v0

v2 whole, which is shorter than its diff:
```python
import jax
import jax.numpy as jnp
from jax import lax
from jax.experimental import pallas as pl
from jax.experimental.pallas import tpu as pltpu
from jax.sharding import PartitionSpec as P

MESH = pl.DeviceIdType.MESH
F32 = jnp.float32
BF16 = jnp.bfloat16

D = 3584
FF = 512
TOK = 128
TOP = 8
CAP = 6
NE = 32
NY = 4
NC = 7
CW = D // NC
NF = 3
NL = NC - NF
BLK = 16
FB = 48
HB = FB // 2
PR = NE * BLK
FR = NE * FB
SR = NE * CAP
ROWS = NY * SR
SL = 0
AL = SL + NL * PR
SF = AL + NL * PR
AF = SF + NF * FR
TB = AF + NF * FR
ST = TB + NF * 2 * NY * TOK
SA_ROWS = ST + 3 * CW
STAGE = AF + FR


def mo(v, m):
    return pl.multiple_of(v, m)


def nn(a, b):
    return lax.dot_general(a, b, (((1,), (0,)), ((), ())), preferred_element_type=F32)


def nt(a, b):
    return lax.dot_general(a, b, (((1,), (1,)), ((), ())), preferred_element_type=F32)


def tn(a, b):
    return lax.dot_general(a, b, (((0,), (0,)), ((), ())), preferred_element_type=F32)


def columns(c):
    return pl.ds(mo(c * CW, CW), CW)


def split3(v):
    a = v.astype(BF16)
    r = v - a.astype(F32)
    b = r.astype(BF16)
    return a, b, (r - b.astype(F32)).astype(BF16)


def kernel(
    tok, probs, ids, cot, wg_hbm, wu_hbm, wd_hbm,
    lo_hbm, gt_hbm, gp_out, gg_hbm, gu_hbm, gd_hbm,
    sa, gath, wg, wu, wd, accg, accu, acch, hid, ggi, gui,
    relay, vrec, relayf, vrecf, back, backf,
    gsel, psel, wout, pack, zacc, sel, pf, perm, zlane, idy, pry, zbuf,
    wsem, asend, arecv, ysend, yrecv, rsend, rrecv, bsend, brecv, gsem, osem, tsend, trecv, zsend, zrecv,
):
    y = lax.axis_index("dp")
    e = lax.axis_index("expert")
    right, left, across = lax.rem(y + 1, NY), lax.rem(y + 3, NY), lax.rem(y + 2, NY)
    sides = (right, left)
    ex, ez, ec = e // 8, lax.rem(e // 2, 4), lax.rem(e, 2)

    def peer(j):
        jx, jz, jc = lax.rem(j, 4), lax.rem(j // 4 + j, 4), j // 16
        return lax.rem(ex + jx, 4) * 8 + lax.rem(ez + jz, 4) * 2 + lax.rem(ec + jc, 2)

    barrier = pltpu.get_barrier_semaphore()
    for other in (right, left, across):
        pl.semaphore_signal(barrier, inc=1, device_id=(other, e), device_id_type=MESH)

    def greet(j, carry):
        pl.semaphore_signal(barrier, inc=1, device_id=(y, peer(j)), device_id_type=MESH)
        return carry

    lax.fori_loop(1, NE, greet, 0)

    def chunk_of(u):
        out = jnp.where(u < 2, u, jnp.where(u == 6, 2, u + 1))
        j = u - NC
        home = jnp.where(lax.rem(j, 2) == 0, NF + j // 2, (j - 1) // 2)
        return jnp.where(u < NC, out, home)

    def weight_copies(u):
        cols = columns(chunk_of(u))
        b = lax.rem(u, 2)
        return (
            pltpu.make_async_copy(wg_hbm.at[cols], wg.at[b], wsem.at[0, b]),
            pltpu.make_async_copy(wu_hbm.at[cols], wu.at[b], wsem.at[1, b]),
            pltpu.make_async_copy(wd_hbm.at[:, cols], wd.at[b], wsem.at[2, b]),
        )

    def load_weights(u):
        for c in weight_copies(u):
            c.start()

    load_weights(0)
    load_weights(1)

    def trow(n, kind, yy):
        return pl.ds(mo(TB + n * (2 * NY * TOK) + kind * (NY * TOK) + yy * TOK, TOK), TOK)

    def first_copy(n, kind, d):
        return pltpu.make_async_remote_copy(
            (tok, cot)[kind].at[:, columns(n)], sa.at[trow(n, kind, y)],
            ysend.at[d, kind, n], yrecv.at[d, kind, n], device_id=(sides[d], e), device_id_type=MESH,
        )

    def first_pass(n, d):
        ref = sa.at[trow(n, d, (left, right)[d])]
        return pltpu.make_async_remote_copy(
            ref, ref, ysend.at[d, 2, n], yrecv.at[d, 2, n], device_id=(sides[d], e), device_id_type=MESH,
        )

    def table_copies():
        return [
            pltpu.make_async_remote_copy(
                src, dst.at[y], tsend.at[k, t], trecv.at[k, t],
                device_id=((right, left, across)[t], e), device_id_type=MESH,
            )
            for t in range(3)
            for k, (src, dst) in enumerate(((ids, idy), (probs, pry)))
        ]

    pl.semaphore_wait(barrier, NE + 2)

    def start_first(n, carry):
        for kind in range(2):
            for d in range(2):
                first_copy(n, kind, d).start()
        return carry

    lax.fori_loop(0, NF, start_first, 0)
    for c in table_copies():
        c.start()

    esub = lax.broadcasted_iota(jnp.int32, (NE, TOK), 0)
    lane = lax.broadcasted_iota(jnp.int32, (TOK, TOK), 1)
    sub = lax.broadcasted_iota(jnp.int32, (TOK, TOK), 0)
    before = jnp.where(sub < lane, 1.0, 0.0).astype(BF16)

    def routing(ids_v, probs_v):
        named = jnp.zeros((NE, TOK), F32)
        weight = jnp.zeros((NE, TOK), F32)
        for k in range(TOP):
            hit = ids_v[k : k + 1, :] == esub
            named = named + jnp.where(hit, 1.0, 0.0)
            weight = weight + jnp.where(hit, probs_v[k : k + 1, :], 0.0)
        rank = nn(named.astype(BF16), before)
        return jnp.where(named > 0.5, rank, 255.0), weight

    def spread_rows(v, count):
        return jnp.broadcast_to(v[:, None, :], (NE, count, TOK)).reshape(NE * count, TOK)

    code0, weight0 = routing(ids[...], probs[...])
    code = spread_rows(code0, BLK)
    weight = spread_rows(weight0, BLK)
    place = lax.rem(lax.broadcasted_iota(jnp.int32, (PR, TOK), 0), BLK)
    slot = place.astype(F32)
    sel_x = jnp.where((place < CAP) & (code == slot), 1.0, 0.0)
    sel_c = jnp.where((place >= CAP) & (place < 2 * CAP) & (code == slot - CAP), 1.0, 0.0)
    gsel[0] = sel_x.astype(BF16)
    gsel[1] = sel_c.astype(BF16)
    psel[...] = jnp.broadcast_to(jnp.sum(sel_c * weight, axis=1, keepdims=True), (PR, TOK))

    def plane_send(src, dst, size, send_sem, recv_sem):
        def send(j, carry):
            t = peer(j)
            pltpu.make_async_remote_copy(
                src(t), dst, send_sem, recv_sem, device_id=(y, t), device_id_type=MESH
            ).start()
            return carry

        lax.fori_loop(1, NE, send, 0)

    def wait_plane(size, sem):
        blocks = sa.at[pl.ds(0, (NE - 1) * size)]
        pltpu.make_async_copy(blocks, blocks, sem).wait()

    def plane_out(l, carry):
        c = NF + l
        rows = nn(gsel[0], tok[:, columns(c)])
        crow = nn(gsel[1], cot[:, columns(c)])
        base = SL + l * PR
        sa[pl.ds(mo(base, PR), PR), :] = (rows + psel[:, 0:1] * crow).astype(BF16)
        mine = pl.ds(mo(AL + l * PR + e * BLK, BLK), BLK)
        sa[mine, :] = sa[pl.ds(mo(base + e * BLK, BLK), BLK), :]
        plane_send(
            lambda t: sa.at[pl.ds(mo(base + t * BLK, BLK), BLK)], sa.at[mine], BLK, asend.at[c], arecv.at[c]
        )
        return carry

    lax.fori_loop(0, NL, plane_out, 0)

    r_i = lax.broadcasted_iota(jnp.int32, (2 * SR, TOK), 0)
    q_i = lax.broadcasted_iota(jnp.int32, (2 * SR, TOK), 1)
    kind_i = jnp.where(r_i >= SR, 1, 0)
    r_i = r_i - kind_i * SR
    src_i = r_i // CAP
    target = src_i * BLK + kind_i * CAP + (r_i - src_i * CAP)
    for b in range(PR // TOK):
        pack[:, b * TOK : (b + 1) * TOK] = jnp.where(q_i + b * TOK == target, 1.0, 0.0).astype(BF16)
    zacc[...] = jnp.zeros((PR, TOK), F32)
    zlane[...] = jnp.zeros((ROWS, TOK), F32)

    def own_copy(c, kind, d):
        ref = gath.at[c, kind, y]
        return pltpu.make_async_remote_copy(
            ref, ref, ysend.at[d, kind, c], yrecv.at[d, kind, c], device_id=(sides[d], e), device_id_type=MESH,
        )

    def pass_copy(c, d):
        ref = gath.at[c, d, (left, right)[d]]
        return pltpu.make_async_remote_copy(
            ref, ref, ysend.at[d, 2, c], yrecv.at[d, 2, c], device_id=(sides[d], e), device_id_type=MESH,
        )

    def early(i, carry):
        @pl.when(i < NF)
        def _():
            for d in range(2):
                first_copy(i, d, d).wait_recv()
                first_pass(i, d).start()
            for d in range(2):
                first_copy(i, 1 - d, d).wait_recv()
            sa[trow(i, 0, y), :] = tok[:, columns(i)]
            sa[trow(i, 1, y), :] = cot[:, columns(i)]

        c = NF + i
        wait_plane(BLK, arecv.at[c])
        both = nn(pack[...], sa[pl.ds(mo(AL + i * PR, PR), PR), :]).astype(BF16)
        gath[c, 0, y] = both[:SR]
        gath[c, 1, y] = both[SR:]
        for kind in range(2):
            for d in range(2):
                own_copy(c, kind, d).start()
        return carry

    lax.fori_loop(0, NL, early, 0)

    for c in table_copies():
        c.wait_recv()
    idy[y] = ids[...]
    pry[y] = probs[...]
    fr_i = lax.rem(lax.broadcasted_iota(jnp.int32, (ROWS, TOK), 0), HB)
    p_rows = jnp.zeros((ROWS, 1), F32)
    for yy in range(NY):
        code_y, weight_y = routing(idy[yy], pry[yy])
        here = (fr_i >= yy * CAP) & (fr_i < (yy + 1) * CAP)
        one = jnp.where(here & (spread_rows(code_y, HB) == (fr_i - yy * CAP).astype(F32)), 1.0, 0.0)
        sel[:, yy * TOK : (yy + 1) * TOK] = one.astype(BF16)
        p_rows = p_rows + jnp.sum(one * spread_rows(weight_y, HB), axis=1, keepdims=True)
    pf[...] = jnp.broadcast_to(p_rows, (ROWS, TOK))

    def build_first(n, carry):
        for d in range(2):
            first_pass(n, d).wait_recv()
        mine = pl.ds(mo(AF + n * FR + e * FB, BLK), FB)
        base = SF + n * FR
        tx = sa[pl.ds(mo(TB + n * (2 * NY * TOK), TOK), NY * TOK), :]
        tc = sa[pl.ds(mo(TB + n * (2 * NY * TOK) + NY * TOK, TOK), NY * TOK), :]

        def quarter(q, carry2):
            rows = pl.ds(mo(q * SR, SR), SR)
            xr = nn(sel[rows, :], tx).reshape(8, HB, CW)
            cr = (pf[rows, 0:1] * nn(sel[rows, :], tc)).reshape(8, HB, CW)
            both = jnp.concatenate([xr, cr], axis=1).reshape(8 * FB, CW)
            sa[pl.ds(mo(base + q * (8 * FB), BLK), 8 * FB), :] = both.astype(BF16)
            return carry2

        lax.fori_loop(0, 4, quarter, 0)
        sa[mine, :] = sa[pl.ds(mo(base + e * FB, BLK), FB), :]
        plane_send(
            lambda t: sa.at[pl.ds(mo(base + t * FB, BLK), FB)], sa.at[mine], FB, asend.at[n], arecv.at[n]
        )
        return carry

    lax.fori_loop(0, NF, build_first, 0)

    r_i = lax.broadcasted_iota(jnp.int32, (ROWS, TOK), 0)
    q_i = lax.broadcasted_iota(jnp.int32, (ROWS, TOK), 1)
    y_i = r_i // SR
    r_i = r_i - y_i * SR
    src_i = r_i // CAP
    target = src_i * HB + y_i * CAP + (r_i - src_i * CAP)
    for b in range(ROWS // TOK):
        perm[:, b * TOK : (b + 1) * TOK] = jnp.where(q_i + b * TOK == target, 1.0, 0.0).astype(BF16)
    by_token = (sel_x * weight).T
    high = by_token.astype(BF16)
    wout[0] = high
    wout[1] = (by_token - high.astype(F32)).astype(BF16)
    wout[2] = sel_c.T.astype(BF16)
    accg[...] = jnp.zeros((ROWS, FF), F32)
    accu[...] = jnp.zeros((ROWS, FF), F32)
    acch[...] = jnp.zeros((ROWS, FF), F32)

    def halves(ref_rows, count):
        v = ref_rows.astype(F32).reshape(count, FB, CW)
        return v[:, :HB].reshape(count * HB, CW), v[:, HB:].reshape(count * HB, CW)

    def gather_step(u, carry):
        c = chunk_of(u)

        @pl.when(u < 2)
        def _():
            for h in range(2):
                l = NF + 2 * u + h
                for d in range(2):
                    own_copy(l, d, d).wait_recv()
                    pass_copy(l, d).start()
                for d in range(2):
                    own_copy(l, 1 - d, d).wait_recv()

        @pl.when((u < 2) | (u == 6))
        def _():
            wait_plane(FB, arecv.at[c])
            xs, cs = [], []
            for h in range(2):
                a, b = halves(sa[pl.ds(mo(AF + c * FR + h * (FR // 2), BLK), FR // 2), :], NE // 2)
                xs.append(a.astype(BF16))
                cs.append(b.astype(BF16))
            for kind, pieces in enumerate((xs, cs)):
                for h in range(2):
                    p = perm[h * 2 * SR : (h + 1) * 2 * SR, :]
                    rows = nn(p[:, : 2 * SR], pieces[0]) + nn(p[:, 2 * SR :], pieces[1])
                    gath[c, kind, 2 * h : 2 * h + 2] = rows.astype(BF16).reshape(2, SR, CW)

        @pl.when((u >= 2) & (u < 6))
        def _():
            for d in range(2):
                pass_copy(c, d).wait_recv()

        for w in weight_copies(u):
            w.wait()
        b = lax.rem(u, 2)

        def half(h, carry2):
            rows = pl.ds(mo(h * 2 * SR, 2 * SR), 2 * SR)
            xr = gath[c, 0, pl.ds(2 * h, 2)].reshape(2 * SR, CW)
            cr = gath[c, 1, pl.ds(2 * h, 2)].reshape(2 * SR, CW)
            accg[rows, :] += nn(xr, wg[b])
            accu[rows, :] += nn(xr, wu[b])
            acch[rows, :] += nt(cr, wd[b])
            return carry2

        lax.fori_loop(0, 2, half, 0)
        load_weights(u + 2)
        return carry

    lax.fori_loop(0, NC, gather_step, 0)

    def activate(i, carry):
        rows = pl.ds(mo(i * 32, 32), 32)
        g, u, h = accg[rows, :], accu[rows, :], acch[rows, :]
        s = jax.nn.sigmoid(g)
        act = g * s
        hid[rows, :] = (act * u).astype(BF16)
        gui[rows, :] = (h * act).astype(BF16)
        ggi[rows, :] = (h * u * s * (1.0 + g * (1.0 - s))).astype(BF16)
        return carry

    lax.fori_loop(0, ROWS // 32, activate, 0)

    def drain_plane(l, carry):
        wait_plane(BLK, asend.at[NF + l])
        return carry

    lax.fori_loop(0, NL, drain_plane, 0)

    def drain_early(n, carry):
        for d in range(2):
            for kind in range(2):
                first_copy(n, kind, d).wait_send()
            first_pass(n, d).wait_send()
        return carry

    lax.fori_loop(0, NF, drain_early, 0)

    def part_base(l):
        return jnp.where(l < 2, l * (2 * ROWS), AF + (l - 2) * (2 * ROWS))

    def part(l, kind, b):
        return pl.ds(mo(part_base(l) + kind * ROWS + b * SR, BLK), SR)

    def relay_copy(l, d):
        c = NF + l
        return pltpu.make_async_remote_copy(
            sa.at[part(l, d, across)], relay.at[l, d], rsend.at[d, 2, c], rrecv.at[d, 2, c],
            device_id=(sides[d], e), device_id_type=MESH,
        )

    def final_copy(l, kind, d):
        c = NF + l
        return pltpu.make_async_remote_copy(
            sa.at[part(l, kind, sides[d])], vrec.at[l, d, kind], rsend.at[d, kind, c], rrecv.at[d, kind, c],
            device_id=(sides[d], e), device_id_type=MESH,
        )

    def fpart(n, kind, b):
        return pl.ds(mo(SF + n * FR + b * (2 * TOK) + kind * TOK, TOK), TOK)

    def relay_first(n, d):
        return pltpu.make_async_remote_copy(
            sa.at[fpart(n, d, across)], relayf.at[n, d], rsend.at[d, 2, n], rrecv.at[d, 2, n],
            device_id=(sides[d], e), device_id_type=MESH,
        )

    def final_first(n, kind, d):
        return pltpu.make_async_remote_copy(
            sa.at[fpart(n, kind, sides[d])], vrecf.at[n, d, kind], rsend.at[d, kind, n], rrecv.at[d, kind, n],
            device_id=(sides[d], e), device_id_type=MESH,
        )

    def add_relay(l):
        for d in range(2):
            relay_copy(l, d).wait_recv()
            rows = part(l, d, sides[d])
            sa[rows, :] = (sa[rows, :].astype(F32) + relay[l, d].astype(F32)).astype(BF16)
            final_copy(l, d, d).start()

    def parts_step(j, carry):
        u = NC + j
        for w in weight_copies(u):
            w.wait()
        b = lax.rem(u, 2)
        plane_first = lax.rem(j, 2) == 0
        base = jnp.where(plane_first, part_base(j // 2), STAGE)

        def half(h, carry2):
            rows = pl.ds(mo(h * 2 * SR, 2 * SR), 2 * SR)
            at = base + h * 2 * SR
            sa[pl.ds(mo(at, BLK), 2 * SR), :] = nn(hid[rows, :], wd[b]).astype(BF16)
            dx = nt(ggi[rows, :], wg[b]) + nt(gui[rows, :], wu[b])
            sa[pl.ds(mo(at + ROWS, BLK), 2 * SR), :] = dx.astype(BF16)
            return carry2

        lax.fori_loop(0, 2, half, 0)

        @pl.when(u + 2 < 2 * NC)
        def _():
            load_weights(u + 2)

        @pl.when(plane_first)
        def _():
            l = j // 2
            for d in range(2):
                relay_copy(l, d).start()
            for d in range(2):
                final_copy(l, 1 - d, d).start()

        @pl.when(lax.rem(j, 2) == 1)
        def _():
            n = (j - 1) // 2
            wait_plane(FB, asend.at[n])
            first = SF + n * FR
            out_rows = sa[pl.ds(STAGE, ROWS), :]
            dx_rows = sa[pl.ds(STAGE + ROWS, ROWS), :]
            for h in range(2):
                p = perm[:, h * 2 * SR : (h + 1) * 2 * SR]
                o = tn(p, out_rows).reshape(NE // 2, HB, CW)
                d = tn(p, dx_rows).reshape(NE // 2, HB, CW)
                both = jnp.concatenate([o, d], axis=1).reshape(FR // 2, CW)
                sa[pl.ds(mo(first + h * (FR // 2), BLK), FR // 2), :] = both.astype(BF16)
            mine = pl.ds(mo(e * FB, BLK), FB)
            backf[n, mine, :] = sa[pl.ds(mo(first + e * FB, BLK), FB), :]
            plane_send(
                lambda t: sa.at[pl.ds(mo(first + t * FB, BLK), FB)], backf.at[n, mine], FB,
                bsend.at[n], brecv.at[n],
            )
            add_relay(n)

        return carry

    lax.fori_loop(0, NC, parts_step, 0)
    add_relay(NL - 1)

    def back_base(l):
        return jnp.where(l < 3, STAGE + 2 * ROWS + l * PR, 4 * ROWS)

    def to_plane(l):
        c = NF + l
        for d in range(2):
            for kind in range(2):
                final_copy(l, kind, d).wait_recv()
        total = []
        for kind in range(2):
            own = sa[part(l, kind, y), :].astype(F32)
            total.append((own + vrec[l, 0, kind].astype(F32) + vrec[l, 1, kind].astype(F32)).astype(BF16))
        base = back_base(l)
        spread = tn(pack[:SR, :], total[0]) + tn(pack[SR:, :], total[1])
        sa[pl.ds(mo(base, BLK), PR), :] = spread.astype(BF16)
        mine = pl.ds(mo(e * BLK, BLK), BLK)
        back[l, mine, :] = sa[pl.ds(mo(base + e * BLK, BLK), BLK), :]
        plane_send(
            lambda t: sa.at[pl.ds(mo(base + t * BLK, BLK), BLK)], back.at[l, mine], BLK, bsend.at[c], brecv.at[c]
        )

    def sum_tokens(n):
        wait_plane(FB, brecv.at[n])
        wait_plane(FB, bsend.at[n])
        tc = sa[pl.ds(mo(TB + n * (2 * NY * TOK) + NY * TOK, TOK), NY * TOK), :]
        lo = jnp.zeros((NY * TOK, CW), F32)
        gt = jnp.zeros((NY * TOK, CW), F32)
        for h in range(2):
            o, d = halves(backf[n, h * (FR // 2) : (h + 1) * (FR // 2), :], NE // 2)
            rows = slice(h * 2 * SR, (h + 1) * 2 * SR)
            s = sel[rows, :]
            prod = nn(s, tc) * o
            z = prod[:, :TOK]
            for q in range(1, CW // TOK):
                z = z + prod[:, q * TOK : (q + 1) * TOK]
            zlane[rows, :] += z
            lo = lo + tn(s, (pf[rows, 0:1] * o).astype(BF16))
            gt = gt + tn(s, d.astype(BF16))
        for yy in range(NY):
            sa[fpart(n, 0, yy), :] = lo[yy * TOK : (yy + 1) * TOK].astype(BF16)
            sa[fpart(n, 1, yy), :] = gt[yy * TOK : (yy + 1) * TOK].astype(BF16)
        for d in range(2):
            relay_first(n, d).start()
        for d in range(2):
            final_first(n, 1 - d, d).start()

    def staged(m, k):
        return pl.ds(mo(jnp.where(lax.rem(m, 2) == 0, ST + k * CW, TB + k * (2 * NY * TOK)), CW), CW)

    def grad_copies(m):
        cols = columns(m)
        return (
            pltpu.make_async_copy(sa.at[staged(m, 0)], gg_hbm.at[cols], gsem.at[0, m]),
            pltpu.make_async_copy(sa.at[staged(m, 1)], gu_hbm.at[cols], gsem.at[1, m]),
            pltpu.make_async_copy(sa.at[staged(m, 2)], gd_hbm.at[:, cols], gsem.at[2, m]),
        )

    def scatter_step(i, carry):
        @pl.when((lax.rem(i, 2) == 1) & (i < 6))
        def _():
            sum_tokens((i - 1) // 2)

        @pl.when((lax.rem(i, 2) == 0) & (i >= 2))
        def _():
            n = i // 2 - 1
            for d in range(2):
                relay_first(n, d).wait_recv()
                rows = fpart(n, d, sides[d])
                sa[rows, :] = (sa[rows, :].astype(F32) + relayf[n, d].astype(F32)).astype(BF16)
                final_first(n, d, d).start()

        @pl.when(i < NL)
        def _():
            to_plane(i)

        @pl.when(i >= 2)
        def _():
            for c in grad_copies(i - 2):
                c.wait()

        xr = gath[i, 0].reshape(ROWS, CW)
        sa[staged(i, 0), :] = tn(xr, ggi[...]).astype(BF16)
        sa[staged(i, 1), :] = tn(xr, gui[...]).astype(BF16)
        sa[staged(i, 2), :] = tn(hid[...], gath[i, 1].reshape(ROWS, CW)).astype(BF16)
        for c in grad_copies(i):
            c.start()
        return carry

    lax.fori_loop(0, NC, scatter_step, 0)

    def score_copies():
        return [
            pltpu.make_async_remote_copy(
                zbuf.at[3], zbuf.at[t], zsend.at[t], zrecv.at[t],
                device_id=((right, left, across)[t], e), device_id_type=MESH,
            )
            for t in range(3)
        ]

    ones = jnp.ones((8, TOK), BF16)
    z0, z1, z2 = split3(zlane[...])
    zbuf[3] = nt(ones, z0) + nt(ones, z1) + nt(ones, z2)
    for c in score_copies():
        c.start()

    def result_copy(blocks, c, kind):
        out = (lo_hbm, gt_hbm)[kind].at[:, columns(c)]
        return pltpu.make_async_copy(blocks.at[pl.ds(kind * TOK, TOK)], out, osem.at[kind, c])

    def last_first(n, carry):
        for d in range(2):
            for kind in range(2):
                final_first(n, kind, d).wait_recv()
        for kind in range(2):
            own = sa[fpart(n, kind, y), :].astype(F32)
            total = own + vrecf[n, 0, kind].astype(F32) + vrecf[n, 1, kind].astype(F32)
            backf[n, kind * TOK : (kind + 1) * TOK, :] = total.astype(BF16)
            result_copy(backf.at[n], n, kind).start()
        return carry

    lax.fori_loop(0, NF - 1, last_first, 0)

    def last_plane(l, carry):
        c = NF + l
        wait_plane(BLK, brecv.at[c])
        blocks = back[l]
        lo = nn(wout[0], blocks) + nn(wout[1], blocks)
        gt = nn(wout[2], blocks)
        zacc[...] += nt(blocks, cot[:, columns(c)])
        for kind, v in enumerate((lo, gt)):
            back[l, kind * TOK : (kind + 1) * TOK, :] = v.astype(BF16)
            result_copy(back.at[l], c, kind).start()
        return carry

    lax.fori_loop(0, NL, last_plane, 0)
    lax.fori_loop(NF - 1, NF, last_first, 0)

    for c in score_copies():
        c.wait_recv()
    zrow = (zbuf[3] + zbuf[0]) + (zbuf[1] + zbuf[2])
    zrow = jnp.broadcast_to(zrow[0:1], (NE, ROWS))
    group = lax.broadcasted_iota(jnp.int32, (NE, ROWS), 1) - HB * lax.broadcasted_iota(jnp.int32, (NE, ROWS), 0)
    z0, z1, z2 = split3(jnp.where((group >= 0) & (group < HB), zrow, 0.0))
    mine = sel[:, pl.ds(mo(y * TOK, TOK), TOK)]
    score = nn(z0, mine) + nn(z1, mine) + nn(z2, mine)
    score = score + jnp.sum((zacc[...] * gsel[0].astype(F32)).reshape(NE, BLK, TOK), axis=1)
    for k in range(TOP):
        gp_out[k : k + 1, :] = jnp.sum(jnp.where(ids[k : k + 1, :] == esub, score, 0.0), axis=0, keepdims=True)

    def drain(c, carry):
        for d in range(2):
            for kind in range(2):
                own_copy(c, kind, d).wait_send()
                final_copy(c - NF, kind, d).wait_send()
            pass_copy(c, d).wait_send()
            relay_copy(c - NF, d).wait_send()
        wait_plane(BLK, bsend.at[c])
        for kind in range(2):
            result_copy(back.at[c - NF], c, kind).wait()
        return carry

    lax.fori_loop(NF, NC, drain, 0)

    def drain_first(n, carry):
        for d in range(2):
            for kind in range(2):
                final_first(n, kind, d).wait_send()
            relay_first(n, d).wait_send()
        for kind in range(2):
            result_copy(backf.at[n], n, kind).wait()
        return carry

    lax.fori_loop(0, NF, drain_first, 0)
    for c in table_copies() + score_copies():
        c.wait_send()
    for m in range(NC - 2, NC):
        for c in grad_copies(m):
            c.wait()


def on_device(tokens, gate_probs, expert_ids, cotangent, w_gate, w_up, w_down):
    vm = pl.BlockSpec(memory_space=pltpu.VMEM)
    hbm = pl.BlockSpec(memory_space=pl.ANY)
    dma = pltpu.SemaphoreType.DMA
    flops = 9 * 2 * ROWS * D * FF
    lo, gt, gp, gg, gu, gd = pl.pallas_call(
        kernel,
        out_shape=(
            jax.ShapeDtypeStruct((TOK, D), BF16),
            jax.ShapeDtypeStruct((TOK, D), BF16),
            jax.ShapeDtypeStruct((TOP, TOK), F32),
            jax.ShapeDtypeStruct((D, FF), BF16),
            jax.ShapeDtypeStruct((D, FF), BF16),
            jax.ShapeDtypeStruct((FF, D), BF16),
        ),
        in_specs=[vm, vm, vm, vm, hbm, hbm, hbm],
        out_specs=(hbm, hbm, vm, hbm, hbm, hbm),
        scratch_shapes=[
            pltpu.VMEM((SA_ROWS, CW), BF16),
            pltpu.VMEM((NC, 2, NY, SR, CW), BF16),
            pltpu.VMEM((2, CW, FF), BF16),
            pltpu.VMEM((2, CW, FF), BF16),
            pltpu.VMEM((2, FF, CW), BF16),
            pltpu.VMEM((ROWS, FF), F32),
            pltpu.VMEM((ROWS, FF), F32),
            pltpu.VMEM((ROWS, FF), F32),
            pltpu.VMEM((ROWS, FF), BF16),
            pltpu.VMEM((ROWS, FF), BF16),
            pltpu.VMEM((ROWS, FF), BF16),
            pltpu.VMEM((NL, 2, SR, CW), BF16),
            pltpu.VMEM((NL, 2, 2, SR, CW), BF16),
            pltpu.VMEM((NF, 2, TOK, CW), BF16),
            pltpu.VMEM((NF, 2, 2, TOK, CW), BF16),
            pltpu.VMEM((NL, PR, CW), BF16),
            pltpu.VMEM((NF, FR, CW), BF16),
            pltpu.VMEM((2, PR, TOK), BF16),
            pltpu.VMEM((PR, TOK), F32),
            pltpu.VMEM((3, TOK, PR), BF16),
            pltpu.VMEM((2 * SR, PR), BF16),
            pltpu.VMEM((PR, TOK), F32),
            pltpu.VMEM((ROWS, NY * TOK), BF16),
            pltpu.VMEM((ROWS, TOK), F32),
            pltpu.VMEM((ROWS, ROWS), BF16),
            pltpu.VMEM((ROWS, TOK), F32),
            pltpu.VMEM((NY, TOP, TOK), jnp.int32),
            pltpu.VMEM((NY, TOP, TOK), F32),
            pltpu.VMEM((4, 8, ROWS), F32),
            dma((3, 2)), dma((NC,)), dma((NC,)),
            dma((2, 3, NC)), dma((2, 3, NC)), dma((2, 3, NC)), dma((2, 3, NC)),
            dma((NC,)), dma((NC,)), dma((3, NC)), dma((2, NC)),
            dma((2, 3)), dma((2, 3)), dma((3,)), dma((3,)),
        ],
        compiler_params=pltpu.CompilerParams(
            collective_id=0, has_side_effects=True, vmem_limit_bytes=int(63.5 * 2**20)
        ),
        cost_estimate=pl.CostEstimate(flops=flops, bytes_accessed=37 * 2**20, transcendentals=ROWS * FF),
    )(tokens, gate_probs.T, expert_ids.T, cotangent, w_gate[0], w_up[0], w_down[0])
    return lo, gt, gp.T, gg[None], gu[None], gd[None]


def solution(mesh):
    rows = P(("dp", "expert"), None)
    wide = P("expert", None, "dp")
    tall = P("expert", "dp", None)
    return jax.shard_map(
        on_device,
        mesh=mesh,
        in_specs=(rows, rows, rows, rows, wide, wide, tall),
        out_specs=(rows, rows, rows, wide, wide, tall),
        check_vma=False,
    )
```

time: 480 us -> 199 us (0.41)
  waiting for transfers between devices: 260 us -> 0 us
  Pallas kernels: 0 us -> 183 us
  local copies, waits for them, and re-layouts: 99 us -> 13.6 us
  matrix products: 59.2 us -> 0 us
  starting transfers between devices: 35.3 us -> 0 us
  other arithmetic: 23.5 us -> 0 us
    all_to_all x4 -> x0, waiting for transfers between devices: 260 us -> none  [the longest x1 73.9 us: on_device(): lax.all_to_all(fanned_x, ('dp', 'expert'), split_axis=0, concat_axis=0, t...]
    pallas_call x0 -> x1, Pallas kernels: none -> 183 us  [on_device(): pl.pallas_call(kernel, out_shape=(jax.ShapeDtypeStruct((TOK, D), BF16), j...]
    dot_general x11 -> x0, matrix products: 59.2 us -> none  [the longest x3 19 us: contract_first(): lax.dot_general(left, right, (((0,), (0,)), ((), ())), preferred_element_...]
    all_to_all x6 -> x0, local copies, waits for them, and re-layouts: 57.6 us -> none  [the longest x2 19.3 us: on_device(): lax.all_to_all(fanned_x, ('dp', 'expert'), split_axis=0, concat_axis=0, t...]
    all_to_all x4 -> x0, starting transfers between devices: 35.3 us -> none  [the longest x1 11.9 us: on_device(): lax.all_to_all(fanned_x, ('dp', 'expert'), split_axis=0, concat_axis=0, t...]
    convert_element_type x2 -> x0, local copies, waits for them, and re-layouts: 21.8 us -> none  [the longest x1 10.9 us: on_device(): returned_dx.astype(jnp.float32)]
    reduce_sum x4 -> x0, other arithmetic: 12.6 us -> none  [the longest x1 5.41 us: on_device(): jnp.sum(returned.astype(jnp.float32).reshape(groups, experts * capacity,...]
    unnamed x21 -> x14, local copies, waits for them, and re-layouts: 1.59 us -> 13.6 us
  transfers between devices with their start and end apart: 4 -> 0, of which waited for: 4 -> 0; matrix products, arithmetic and copies ran while one was open for 15% -> 0% of each run, Pallas kernels for 0% -> 0%
where the time goes in v2:
time: 199 us; the launch traced here: 198 us
  Pallas kernels  183 us (92%)
  local copies, waits for them, and re-layouts  13.6 us (7%)
    pallas_call x1, Pallas kernels, on_device(): pl.pallas_call(kernel, out_shape=(jax.ShapeDtypeStruct((TOK, D), BF16), j...  183 us
    unnamed x14, local copies, waits for them, and re-layouts  13.6 us

profile of v2, /device:TPU:1, one launch (start us, length us, event | category | flops | bytes accessed | tf_op | source)
XLA Modules:
  0.0 197.7 jit_solution(13450983901966965842)
XLA Ops:
  0.6 183.4 %shard_map.118 = (bf16[128,3584]{1,0:T(8,128)(2,1)}, bf16[128,3584]{1,0:T(8,128)(2,1)}, f32[8,128]{1,0:T(8,128)}, bf16[3584,512]{1,0:T(8,128)(2,1)}, bf16[3584,5...) custom-call(bf16[128,3584]{1,0:T(8,128)(2,1)} %tok.1, f32[8,128]{1,0:T(8,128)} %bitcast.16, s32[8,128]{1,0:T(8,128)} %bitcast.17, ...), custom_call_target="tpu_custom_call" | custom-call | flops 25367150592 | bytes 38797312 | tf_op jit(solution)/shard_map/pallas_call | solution.py:679
  184.1 0.0 copy-start.3
  184.1 0.0 copy-start.2
  184.1 2.3 %copy.19 = bf16[128,3584]{1,0:T(8,128)(2,1)} copy(bf16[128,3584]{1,0:T(8,128)(2,1)} %get-tuple-element.24) | data formatting | bytes 1835008
  186.4 2.2 %copy.20 = bf16[128,3584]{1,0:T(8,128)(2,1)} copy(bf16[128,3584]{1,0:T(8,128)(2,1)} %get-tuple-element.25) | data formatting | bytes 1835008
  188.5 0.0 copy-done.3
  188.5 0.6 copy.21
  189.1 0.0 copy-done.2
  189.1 0.0 copy-start.1
  189.1 1.9 copy.22
  191.0 1.5 copy-done.1
  192.5 0.0 copy-start
  192.5 1.9 copy.23
  194.4 1.5 copy-done
  195.9 1.8 copy.24
Async XLA Ops:
  184.1 4.5 %copy-start.3 = (f32[8,128]{1,0:T(8,128)S(1)}, f32[8,128]{1,0:T(8,128)}, u32[]{:S(2)}) copy-start(f32[8,128]{1,0:T(8,128)} %get-tuple-element.14) | copy-start | bytes 12292
  184.1 5.1 %copy-start.2 = (bf16[3584,512]{1,0:T(8,128)(2,1)S(1)}, bf16[3584,512]{1,0:T(8,128)(2,1)}, u32[]{:S(2)}) copy-start(bf16[3584,512]{1,0:T(8,128)(2,1)} %get-tuple-element.15) | copy-start | bytes 11010052
  189.1 3.4 %copy-start.1 = (bf16[3584,512]{1,0:T(8,128)(2,1)S(1)}, bf16[3584,512]{1,0:T(8,128)(2,1)}, u32[]{:S(2)}) copy-start(bf16[3584,512]{1,0:T(8,128)(2,1)} %get-tuple-element.16) | copy-start | bytes 11010052
  192.5 3.4 %copy-start = (bf16[512,3584]{1,0:T(8,128)(2,1)S(1)}, bf16[512,3584]{1,0:T(8,128)(2,1)}, u32[]{:S(2)}) copy-start(bf16[512,3584]{1,0:T(8,128)(2,1)} %get-tuple-element.17) | copy-start | bytes 11010052

commit v3 on v2

v3 whole, which is shorter than its diff:
```python
import jax
import jax.numpy as jnp
from jax import lax
from jax.experimental import pallas as pl
from jax.experimental.pallas import tpu as pltpu
from jax.sharding import PartitionSpec as P

MESH = pl.DeviceIdType.MESH
F32 = jnp.float32
BF16 = jnp.bfloat16

D = 3584
FF = 512
TOK = 128
TOP = 8
CAP = 6
NE = 32
NY = 4
NC = 7
CW = D // NC
NF = 3
NL = NC - NF
BLK = 16
FB = 48
HB = FB // 2
NX = NF + 1
FR = NE * FB
SR = NE * CAP
ROWS = NY * SR
TR = 2 * NY * TOK
AF = NX * FR
TB = 2 * NX * FR
ST = TB + NX * TR
SA_ROWS = ST + 3 * CW
LARGE, PIECES = 5, 4
PB = NF * FR
STAGE = PB + NL * FR


def mo(v, m):
    return pl.multiple_of(v, m)


def nn(a, b):
    return lax.dot_general(a, b, (((1,), (0,)), ((), ())), preferred_element_type=F32)


def nt(a, b):
    return lax.dot_general(a, b, (((1,), (1,)), ((), ())), preferred_element_type=F32)


def tn(a, b):
    return lax.dot_general(a, b, (((0,), (0,)), ((), ())), preferred_element_type=F32)


def columns(c):
    return pl.ds(mo(c * CW, CW), CW)


def split3(v):
    a = v.astype(BF16)
    r = v - a.astype(F32)
    b = r.astype(BF16)
    return a, b, (r - b.astype(F32)).astype(BF16)


def kernel(
    tok_hbm, probs, ids, cot_hbm, wg_hbm, wu_hbm, wd_hbm,
    lo_hbm, gt_hbm, gp_out, gg_hbm, gu_hbm, gd_hbm,
    sa, gath, wg, wu, wd, accg, accu, acch, hid, ggi, gui,
    relay, vrec, relayf, vrecf, backf,
    sel, pf, perm, idy, pry, zbuf, tok, cot,
    wsem, asend, arecv, ysend, yrecv, rsend, rrecv, bsend, brecv, gsem, osem, tsend, trecv, zsend, zrecv, isem,
):
    inputs = (
        pltpu.make_async_copy(tok_hbm, tok, isem.at[0]),
        pltpu.make_async_copy(cot_hbm, cot, isem.at[1]),
    )
    for c in inputs:
        c.start()
    y = lax.axis_index("dp")
    e = lax.axis_index("expert")
    right, left, across = lax.rem(y + 1, NY), lax.rem(y + 3, NY), lax.rem(y + 2, NY)
    sides = (right, left)
    ex, ez, ec = e // 8, lax.rem(e // 2, 4), lax.rem(e, 2)

    def peer(j):
        jx, jz, jc = lax.rem(j, 4), lax.rem(j // 4 + j, 4), j // 16
        return lax.rem(ex + jx, 4) * 8 + lax.rem(ez + jz, 4) * 2 + lax.rem(ec + jc, 2)

    barrier = pltpu.get_barrier_semaphore()
    for other in (right, left, across):
        pl.semaphore_signal(barrier, inc=1, device_id=(other, e), device_id_type=MESH)

    by_x = [lax.rem(ex + j, 4) * 8 for j in range(4)]
    by_z = [lax.rem(ez + j, 4) * 2 for j in range(4)]
    for j in range(1, NE):
        t = by_x[j % 4] + by_z[j // 4 % 4] + (ec if j < 16 else 1 - ec)
        pl.semaphore_signal(barrier, inc=1, device_id=(y, t), device_id_type=MESH)

    def chunk_of(u):
        out = jnp.where(u < 2, u, jnp.where(u == 6, 2, u + 1))
        j = u - NC
        home = jnp.where(lax.rem(j, 2) == 0, NF + j // 2, (j - 1) // 2)
        return jnp.where(u < NC, out, home)

    def weight_copies(u):
        cols = columns(chunk_of(u))
        b = lax.rem(u, 2)
        return (
            pltpu.make_async_copy(wg_hbm.at[cols], wg.at[b], wsem.at[0, b]),
            pltpu.make_async_copy(wu_hbm.at[cols], wu.at[b], wsem.at[1, b]),
            pltpu.make_async_copy(wd_hbm.at[:, cols], wd.at[b], wsem.at[2, b]),
        )

    def load_weights(u):
        for c in weight_copies(u):
            c.start()

    load_weights(0)
    load_weights(1)

    def trow(q, kind, g):
        return pl.ds(mo(TB + q * TR + kind * (NY * TOK) + g * TOK, TOK), TOK)

    def first_copy(n, kind, d):
        return pltpu.make_async_remote_copy(
            (tok, cot)[kind].at[:, columns(n)], sa.at[trow(n, kind, y)],
            ysend.at[d, kind, n], yrecv.at[d, kind, n], device_id=(sides[d], e), device_id_type=MESH,
        )

    def first_pass(n, d):
        ref = sa.at[trow(n, d, (left, right)[d])]
        return pltpu.make_async_remote_copy(
            ref, ref, ysend.at[d, 2, n], yrecv.at[d, 2, n], device_id=(sides[d], e), device_id_type=MESH,
        )

    def table_copies():
        return [
            pltpu.make_async_remote_copy(
                src, dst.at[y], tsend.at[k, t], trecv.at[k, t],
                device_id=((right, left, across)[t], e), device_id_type=MESH,
            )
            for t in range(3)
            for k, (src, dst) in enumerate(((ids, idy), (probs, pry)))
        ]

    def start_first(n, carry):
        for kind in range(2):
            for d in range(2):
                first_copy(n, kind, d).start()
        return carry

    for c in inputs:
        c.wait()
    pl.semaphore_wait(barrier, NE + 2)
    lax.fori_loop(0, NF, start_first, 0)
    for c in table_copies():
        c.start()

    esub = lax.broadcasted_iota(jnp.int32, (NE, TOK), 0)
    lane = lax.broadcasted_iota(jnp.int32, (TOK, TOK), 1)
    sub = lax.broadcasted_iota(jnp.int32, (TOK, TOK), 0)
    before = jnp.where(sub < lane, 1.0, 0.0).astype(BF16)

    def routing(ids_v, probs_v):
        named = jnp.zeros((NE, TOK), F32)
        weight = jnp.zeros((NE, TOK), F32)
        for k in range(TOP):
            hit = ids_v[k : k + 1, :] == esub
            named = named + jnp.where(hit, 1.0, 0.0)
            weight = weight + jnp.where(hit, probs_v[k : k + 1, :], 0.0)
        rank = nn(named.astype(BF16), before)
        return jnp.where(named > 0.5, rank, 255.0), weight

    def spread_rows(v, count):
        return jnp.broadcast_to(v[:, None, :], (NE, count, TOK)).reshape(NE * count, TOK)

    fr_i = lax.rem(lax.broadcasted_iota(jnp.int32, (ROWS, TOK), 0), HB)

    def place(k, tables):
        p_rows = jnp.zeros((ROWS, 1), F32)
        for g, (code_g, weight_g) in enumerate(tables):
            here = (fr_i >= g * CAP) & (fr_i < (g + 1) * CAP)
            one = jnp.where(here & (spread_rows(code_g, HB) == (fr_i - g * CAP).astype(F32)), 1.0, 0.0)
            sel[k, :, g * TOK : (g + 1) * TOK] = one.astype(BF16)
            p_rows = p_rows + jnp.sum(one * spread_rows(weight_g, HB), axis=1, keepdims=True)
        pf[k] = jnp.broadcast_to(p_rows, (ROWS, TOK))

    own_table = routing(ids[...], probs[...])

    def stack(c, carry):
        q, g = jnp.minimum(c, NF), jnp.where(c < NF, y, c - NF)
        sa[trow(q, 0, g), :] = tok[:, columns(c)]
        sa[trow(q, 1, g), :] = cot[:, columns(c)]
        return carry

    lax.fori_loop(NF, NC, stack, 0)
    place(1, [own_table] * NL)

    def plane_send(base, arrival, send_sem, recv_sem):
        def send(j, carry):
            t = peer(j)
            pltpu.make_async_remote_copy(
                sa.at[pl.ds(mo(base + t * FB, BLK), FB)], arrival, send_sem, recv_sem,
                device_id=(y, t), device_id_type=MESH,
            ).start()
            return carry

        lax.fori_loop(1, NE, send, 0)

    def wait_plane(sem):
        blocks = sa.at[pl.ds(0, (NE - 1) * FB)]
        pltpu.make_async_copy(blocks, blocks, sem).wait()

    def build(q, k):
        mine = pl.ds(mo(AF + q * FR + e * FB, BLK), FB)
        base = q * FR
        tx = sa[pl.ds(mo(TB + q * TR, TOK), NY * TOK), :]
        tc = sa[pl.ds(mo(TB + q * TR + NY * TOK, TOK), NY * TOK), :]

        def quarter(i, carry2):
            rows = pl.ds(mo(i * SR, SR), SR)
            xr = nn(sel[k, rows, :], tx).reshape(8, HB, CW)
            cr = (pf[k, rows, 0:1] * nn(sel[k, rows, :], tc)).reshape(8, HB, CW)
            both = jnp.concatenate([xr, cr], axis=1).reshape(8 * FB, CW)
            sa[pl.ds(mo(base + i * (8 * FB), BLK), 8 * FB), :] = both.astype(BF16)
            return carry2

        lax.fori_loop(0, 4, quarter, 0)
        sa[mine, :] = sa[pl.ds(mo(base + e * FB, BLK), FB), :]
        plane_send(base, sa.at[mine], asend.at[q], arecv.at[q])

    build(NF, 1)
    lax.fori_loop(0, NF, stack, 0)

    r_i = lax.broadcasted_iota(jnp.int32, (ROWS, TOK), 0)
    q_i = lax.broadcasted_iota(jnp.int32, (ROWS, TOK), 1)
    y_i = r_i // SR
    r_i = r_i - y_i * SR
    src_i = r_i // CAP
    target = src_i * HB + y_i * CAP + (r_i - src_i * CAP)
    for b in range(ROWS // TOK):
        perm[:, b * TOK : (b + 1) * TOK] = jnp.where(q_i + b * TOK == target, 1.0, 0.0).astype(BF16)
    accg[...] = jnp.zeros((ROWS, FF), F32)
    accu[...] = jnp.zeros((ROWS, FF), F32)
    acch[...] = jnp.zeros((ROWS, FF), F32)

    def own_copy(c, kind, d):
        ref = gath.at[c, kind, y]
        return pltpu.make_async_remote_copy(
            ref, ref, ysend.at[d, kind, c], yrecv.at[d, kind, c], device_id=(sides[d], e), device_id_type=MESH,
        )

    def pass_copy(c, d):
        ref = gath.at[c, d, (left, right)[d]]
        return pltpu.make_async_remote_copy(
            ref, ref, ysend.at[d, 2, c], yrecv.at[d, 2, c], device_id=(sides[d], e), device_id_type=MESH,
        )

    def early(i, carry):
        for d in range(2):
            first_copy(i, d, d).wait_recv()
            first_pass(i, d).start()
        for d in range(2):
            first_copy(i, 1 - d, d).wait_recv()
        return carry

    lax.fori_loop(0, NF, early, 0)

    for c in table_copies():
        c.wait_recv()
    idy[y] = ids[...]
    pry[y] = probs[...]
    place(0, [routing(idy[g], pry[g]) for g in range(NY)])

    def halves(ref_rows, count):
        v = ref_rows.astype(F32).reshape(count, FB, CW)
        return v[:, :HB].reshape(count * HB, CW), v[:, HB:].reshape(count * HB, CW)

    def arrived(q, store):
        wait_plane(arecv.at[q])
        xs, cs = [], []
        for h in range(2):
            a, b = halves(sa[pl.ds(mo(AF + q * FR + h * (FR // 2), BLK), FR // 2), :], NE // 2)
            xs.append(a.astype(BF16))
            cs.append(b.astype(BF16))
        for kind, pieces in enumerate((xs, cs)):
            for h in range(2):
                p = perm[h * 2 * SR : (h + 1) * 2 * SR, :]
                rows = nn(p[:, : 2 * SR], pieces[0]) + nn(p[:, 2 * SR :], pieces[1])
                store(kind, h, rows.astype(BF16).reshape(2, SR, CW))

    def keep_plane(kind, h, rows):
        for i in range(2):
            gath[NF + 2 * h + i, kind, y] = rows[i]

    arrived(NF, keep_plane)
    for c in range(NF, NC):
        for kind in range(2):
            for d in range(2):
                own_copy(c, kind, d).start()

    def build_first(n, carry):
        for d in range(2):
            first_pass(n, d).wait_recv()
        build(n, 0)
        return carry

    lax.fori_loop(0, NF, build_first, 0)

    def gather_step(u, carry):
        c = chunk_of(u)

        @pl.when(u < 2)
        def _():
            for h in range(2):
                l = NF + 2 * u + h
                for d in range(2):
                    own_copy(l, d, d).wait_recv()
                    pass_copy(l, d).start()
                for d in range(2):
                    own_copy(l, 1 - d, d).wait_recv()

        @pl.when(u < 2)
        def _():
            def keep_first(kind, h, rows):
                gath[c, kind, 2 * h : 2 * h + 2] = rows

            arrived(c, keep_first)

        @pl.when(u >= 2)
        def _():
            for d in range(2):
                pass_copy(c, d).wait_recv()

        for w in weight_copies(u):
            w.wait()
        b = lax.rem(u, 2)

        def half(h, carry2):
            rows = pl.ds(mo(h * 2 * SR, 2 * SR), 2 * SR)
            xr = gath[c, 0, pl.ds(2 * h, 2)].reshape(2 * SR, CW)
            cr = gath[c, 1, pl.ds(2 * h, 2)].reshape(2 * SR, CW)
            accg[rows, :] += nn(xr, wg[b])
            accu[rows, :] += nn(xr, wu[b])
            acch[rows, :] += nt(cr, wd[b])
            return carry2

        lax.fori_loop(0, 2, half, 0)
        @pl.when(u + 2 <= NC)
        def _():
            load_weights(u + 2)

        return carry

    lax.fori_loop(0, NC - 1, gather_step, 0)

    def keep_last_first(kind, h, rows):
        gath[NF - 1, kind, 2 * h : 2 * h + 2] = rows

    arrived(NF - 1, keep_last_first)
    for u in (NC - 1, NC):
        for w in weight_copies(u):
            w.wait()
    wait_plane(asend.at[NF])
    now, later = (NC - 1) % 2, NC % 2

    def part_base(l):
        return PB + l * FR

    def part(l, kind, b):
        return pl.ds(mo(part_base(l) + kind * ROWS + b * SR, BLK), SR)

    def relay_copy(l, d):
        c = NF + l
        return pltpu.make_async_remote_copy(
            sa.at[part(l, d, across)], relay.at[l, d], rsend.at[d, 2, c], rrecv.at[d, 2, c],
            device_id=(sides[d], e), device_id_type=MESH,
        )

    def final_copy(l, kind, d):
        c = NF + l
        return pltpu.make_async_remote_copy(
            sa.at[part(l, kind, sides[d])], vrec.at[l, d, kind], rsend.at[d, kind, c], rrecv.at[d, kind, c],
            device_id=(sides[d], e), device_id_type=MESH,
        )

    def fpart(n, kind, b):
        return pl.ds(mo(n * FR + b * (2 * TOK) + kind * TOK, TOK), TOK)

    def relay_first(n, d):
        return pltpu.make_async_remote_copy(
            sa.at[fpart(n, d, across)], relayf.at[n, d], rsend.at[d, 2, n], rrecv.at[d, 2, n],
            device_id=(sides[d], e), device_id_type=MESH,
        )

    def final_first(n, kind, d):
        return pltpu.make_async_remote_copy(
            sa.at[fpart(n, kind, sides[d])], vrecf.at[n, d, kind], rsend.at[d, kind, n], rrecv.at[d, kind, n],
            device_id=(sides[d], e), device_id_type=MESH,
        )

    def add_relay(l):
        for d in range(2):
            relay_copy(l, d).wait_recv()
            rows = part(l, d, sides[d])
            sa[rows, :] = (sa[rows, :].astype(F32) + relay[l, d].astype(F32)).astype(BF16)
            final_copy(l, d, d).start()

    def middle(step, carry):
        b = lax.rem(y + jnp.where(step == 0, 2, jnp.where(step == 2, 3, jnp.where(step == 3, 0, 1))), NY)
        rows = pl.ds(mo(b * SR, SR), SR)
        xr, cr = gath[NF - 1, 0, b], gath[NF - 1, 1, b]
        accg[rows, :] += nn(xr, wg[now])
        accu[rows, :] += nn(xr, wu[now])
        acch[rows, :] += nt(cr, wd[now])

        def activate(i, carry2):
            some = pl.ds(mo(b * SR + i * 32, 32), 32)
            g, u, h = accg[some, :], accu[some, :], acch[some, :]
            s = jax.nn.sigmoid(g)
            act = g * s
            hid[some, :] = (act * u).astype(BF16)
            gui[some, :] = (h * act).astype(BF16)
            ggi[some, :] = (h * u * s * (1.0 + g * (1.0 - s))).astype(BF16)
            return carry2

        lax.fori_loop(0, SR // 32, activate, 0)
        sa[part(0, 0, b), :] = nn(hid[rows, :], wd[later]).astype(BF16)
        sa[part(0, 1, b), :] = (nt(ggi[rows, :], wg[later]) + nt(gui[rows, :], wu[later])).astype(BF16)

        @pl.when(step == 0)
        def _():
            for d in range(2):
                relay_copy(0, d).start()

        for d in range(2):
            @pl.when(step == 1 + d)
            def _():
                final_copy(0, 1 - d, d).start()

        return carry

    lax.fori_loop(0, NY, middle, 0)
    load_weights(NC + 1)
    load_weights(NC + 2)
    accg[:, : 2 * TOK] = jnp.zeros((ROWS, 2 * TOK), F32)

    def drain_early(n, carry):
        for d in range(2):
            for kind in range(2):
                first_copy(n, kind, d).wait_send()
            first_pass(n, d).wait_send()
        return carry

    lax.fori_loop(0, NF, drain_early, 0)

    def send_back(q, base):
        out_rows = sa[pl.ds(STAGE, ROWS), :]
        dx_rows = sa[pl.ds(STAGE + ROWS, ROWS), :]
        for h in range(2):
            p = perm[:, h * 2 * SR : (h + 1) * 2 * SR]
            o = tn(p, out_rows).reshape(NE // 2, HB, CW)
            d = tn(p, dx_rows).reshape(NE // 2, HB, CW)
            both = jnp.concatenate([o, d], axis=1).reshape(FR // 2, CW)
            sa[pl.ds(mo(base + h * (FR // 2), BLK), FR // 2), :] = both.astype(BF16)
        mine = pl.ds(mo(e * FB, BLK), FB)
        backf[q, mine, :] = sa[pl.ds(mo(base + e * FB, BLK), FB), :]
        plane_send(base, backf.at[q, mine], bsend.at[q], brecv.at[q])

    def parts_step(j, carry):
        u = NC + j
        for w in weight_copies(u):
            w.wait()
        b = lax.rem(u, 2)
        plane_first = lax.rem(j, 2) == 0
        base = jnp.where(plane_first, part_base(j // 2), STAGE)

        def half(h, carry2):
            rows = pl.ds(mo(h * 2 * SR, 2 * SR), 2 * SR)
            at = base + h * 2 * SR
            sa[pl.ds(mo(at, BLK), 2 * SR), :] = nn(hid[rows, :], wd[b]).astype(BF16)
            dx = nt(ggi[rows, :], wg[b]) + nt(gui[rows, :], wu[b])
            sa[pl.ds(mo(at + ROWS, BLK), 2 * SR), :] = dx.astype(BF16)
            return carry2

        lax.fori_loop(0, 2, half, 0)

        @pl.when(u + 2 < 2 * NC)
        def _():
            load_weights(u + 2)

        @pl.when(plane_first)
        def _():
            l = j // 2
            for d in range(2):
                relay_copy(l, d).start()
            for d in range(2):
                final_copy(l, 1 - d, d).start()

        @pl.when(lax.rem(j, 2) == 1)
        def _():
            n = (j - 1) // 2
            wait_plane(asend.at[n])
            send_back(n, n * FR)
            add_relay(n)

        return carry

    lax.fori_loop(1, NC, parts_step, 0)
    add_relay(NL - 1)

    def to_plane(l):
        for d in range(2):
            for kind in range(2):
                final_copy(l, kind, d).wait_recv()
        for kind in range(2):
            own = sa[part(l, kind, y), :].astype(F32)
            total = own + vrec[l, 0, kind].astype(F32) + vrec[l, 1, kind].astype(F32)
            sa[pl.ds(mo(STAGE + kind * ROWS + l * SR, BLK), SR), :] = total.astype(BF16)

    def parts_sent(l):
        for d in range(2):
            for kind in range(2):
                final_copy(l, kind, d).wait_send()
            relay_copy(l, d).wait_send()

    def sum_tokens(q, k, store):
        wait_plane(brecv.at[q])
        tc = sa[pl.ds(mo(TB + q * TR + NY * TOK, TOK), NY * TOK), :]
        parts = (slice(0, ROWS // 2), slice(ROWS // 2, ROWS))

        def rows_of(h, kind):
            return halves(backf[q, h * (FR // 2) : (h + 1) * (FR // 2), :], NE // 2)[kind]

        for h, rows in enumerate(parts):
            prod = nn(sel[k, rows, :], tc) * rows_of(h, 0)
            z = prod[:, :TOK]
            for b in range(1, CW // TOK):
                z = z + prod[:, b * TOK : (b + 1) * TOK]
            accg[rows, k * TOK : (k + 1) * TOK] += z
        lo = [(pf[k, rows, 0:1] * rows_of(h, 0)).astype(BF16) for h, rows in enumerate(parts)]
        store(0, tn(sel[k, parts[0], :], lo[0]) + tn(sel[k, parts[1], :], lo[1]))
        gt = [rows_of(h, 1).astype(BF16) for h in range(2)]
        store(1, tn(sel[k, parts[0], :], gt[0]) + tn(sel[k, parts[1], :], gt[1]))

    def sum_first(n):
        wait_plane(bsend.at[n])

        def keep(kind, v):
            for g in range(NY):
                sa[fpart(n, kind, g), :] = v[g * TOK : (g + 1) * TOK].astype(BF16)

        sum_tokens(n, 0, keep)
        for d in range(2):
            relay_first(n, d).start()
        for d in range(2):
            final_first(n, 1 - d, d).start()

    def staged(m, k):
        return pl.ds(mo(jnp.where(lax.rem(m, 2) == 0, ST + k * CW, TB + k * TR), CW), CW)

    def grad_copies(m):
        cols = columns(m)
        return (
            pltpu.make_async_copy(sa.at[staged(m, 0)], gg_hbm.at[cols], gsem.at[0, m]),
            pltpu.make_async_copy(sa.at[staged(m, 1)], gu_hbm.at[cols], gsem.at[1, m]),
            pltpu.make_async_copy(sa.at[staged(m, 2)], gd_hbm.at[:, cols], gsem.at[2, m]),
        )

    def scatter_step(i, carry):
        @pl.when((lax.rem(i, 2) == 1) & (i < 6))
        def _():
            sum_first((i - 1) // 2)

        @pl.when((lax.rem(i, 2) == 0) & (i >= 2))
        def _():
            n = i // 2 - 1
            for d in range(2):
                relay_first(n, d).wait_recv()
                rows = fpart(n, d, sides[d])
                sa[rows, :] = (sa[rows, :].astype(F32) + relayf[n, d].astype(F32)).astype(BF16)
                final_first(n, d, d).start()

        @pl.when(i < NL)
        def _():
            to_plane(i)

        @pl.when(i == NL - 1)
        def _():
            parts_sent(0)
            send_back(NF, PB)

        @pl.when(i >= 2)
        def _():
            for c in grad_copies(i - 2):
                c.wait()

        xr = gath[i, 0].reshape(ROWS, CW)
        sa[staged(i, 0), :] = tn(xr, ggi[...]).astype(BF16)
        sa[staged(i, 1), :] = tn(xr, gui[...]).astype(BF16)
        sa[staged(i, 2), :] = tn(hid[...], gath[i, 1].reshape(ROWS, CW)).astype(BF16)
        for c in grad_copies(i):
            c.start()
        return carry

    lax.fori_loop(0, NC, scatter_step, 0)

    def score_copies():
        return [
            pltpu.make_async_remote_copy(
                zbuf.at[3], zbuf.at[t], zsend.at[t], zrecv.at[t],
                device_id=((right, left, across)[t], e), device_id_type=MESH,
            )
            for t in range(3)
        ]

    ones = jnp.ones((8, TOK), BF16)
    z0, z1, z2 = split3(accg[:, :TOK])
    zbuf[3] = nt(ones, z0) + nt(ones, z1) + nt(ones, z2)
    for c in score_copies():
        c.start()

    def result_copy(n, kind):
        out = (lo_hbm, gt_hbm)[kind].at[:, columns(n)]
        return pltpu.make_async_copy(backf.at[n, pl.ds(kind * TOK, TOK)], out, osem.at[kind, n])

    def last_copy(l, kind):
        rows = pl.ds(mo(STAGE + kind * (NY * TOK) + l * TOK, TOK), TOK)
        return pltpu.make_async_copy(sa.at[rows], (lo_hbm, gt_hbm)[kind].at[:, columns(NF + l)], osem.at[kind, NF + l])

    def last_first(n, carry):
        for d in range(2):
            for kind in range(2):
                final_first(n, kind, d).wait_recv()
        for kind in range(2):
            own = sa[fpart(n, kind, y), :].astype(F32)
            total = own + vrecf[n, 0, kind].astype(F32) + vrecf[n, 1, kind].astype(F32)
            backf[n, kind * TOK : (kind + 1) * TOK, :] = total.astype(BF16)
            result_copy(n, kind).start()
        return carry

    lax.fori_loop(0, NF, last_first, 0)

    def keep_last(kind, v):
        sa[pl.ds(STAGE + kind * NY * TOK, NY * TOK), :] = v.astype(BF16)
        for l in range(NL):
            last_copy(l, kind).start()

    sum_tokens(NF, 1, keep_last)

    for c in score_copies():
        c.wait_recv()
    zrow = (zbuf[3] + zbuf[0]) + (zbuf[1] + zbuf[2])
    group = lax.broadcasted_iota(jnp.int32, (NE, ROWS), 1) - HB * lax.broadcasted_iota(jnp.int32, (NE, ROWS), 0)
    group = (group >= 0) & (group < HB)
    z0, z1, z2 = split3(jnp.where(group, jnp.broadcast_to(zrow[0:1], (NE, ROWS)), 0.0))
    mine = sel[0, :, pl.ds(mo(y * TOK, TOK), TOK)]
    score = nn(z0, mine) + nn(z1, mine) + nn(z2, mine)
    z0, z1, z2 = split3(accg[:, TOK : 2 * TOK])
    zrow = nt(ones, z0) + nt(ones, z1) + nt(ones, z2)
    z0, z1, z2 = split3(jnp.where(group, jnp.broadcast_to(zrow[0:1], (NE, ROWS)), 0.0))
    for l in range(NL):
        mine = sel[1, :, l * TOK : (l + 1) * TOK]
        score = score + (nn(z0, mine) + nn(z1, mine) + nn(z2, mine))
    for k in range(TOP):
        gp_out[k : k + 1, :] = jnp.sum(jnp.where(ids[k : k + 1, :] == esub, score, 0.0), axis=0, keepdims=True)

    def drain(c, carry):
        l = c - NF
        for d in range(2):
            for kind in range(2):
                own_copy(c, kind, d).wait_send()
            pass_copy(c, d).wait_send()
        for kind in range(2):
            last_copy(l, kind).wait()

        @pl.when(l >= 1)
        def _():
            parts_sent(l)

        return carry

    lax.fori_loop(NF, NC, drain, 0)
    wait_plane(bsend.at[NF])

    def drain_first(n, carry):
        for d in range(2):
            for kind in range(2):
                final_first(n, kind, d).wait_send()
            relay_first(n, d).wait_send()
        for kind in range(2):
            result_copy(n, kind).wait()
        return carry

    lax.fori_loop(0, NF, drain_first, 0)
    for c in table_copies() + score_copies():
        c.wait_send()
    for m in range(NC - 2, NC):
        for c in grad_copies(m):
            c.wait()


def keep_kernel(*refs):
    small, small_out = refs[0], refs[LARGE + 1]
    small_out[...] = small[...]
    refs = refs[1 : LARGE + 1] + refs[LARGE + 2 :]
    count = LARGE
    rsem, wsem = refs[-2:]
    reads, writes = [], []
    for k in range(PIECES):
        for i in range(count):
            src, dst, held = refs[i], refs[count + i], refs[2 * count + i]
            step = src.shape[0] // PIECES
            rows = pl.ds(k * step, step)
            reads.append(pltpu.make_async_copy(src.at[rows], held.at[rows], rsem.at[i, k]))
            writes.append(pltpu.make_async_copy(held.at[rows], dst.at[rows], wsem.at[i, k]))
    for c in reads:
        c.start()
    for r, w in zip(reads, writes):
        r.wait()
        w.start()
    for w in writes:
        w.wait()


def keep(small, *arrays):
    vm = pl.BlockSpec(memory_space=pltpu.VMEM)
    hbm = pl.BlockSpec(memory_space=pl.ANY)
    sems = pltpu.SemaphoreType.DMA((LARGE, PIECES))
    return pl.pallas_call(
        keep_kernel,
        out_shape=tuple(jax.ShapeDtypeStruct(a.shape, a.dtype) for a in (small, *arrays)),
        in_specs=[vm] + [hbm] * LARGE,
        out_specs=(vm,) + (hbm,) * LARGE,
        scratch_shapes=[pltpu.VMEM(a.shape, a.dtype) for a in arrays] + [sems, sems],
        compiler_params=pltpu.CompilerParams(vmem_limit_bytes=63 * 2**20),
    )(small, *arrays)


def on_device(tokens, gate_probs, expert_ids, cotangent, w_gate, w_up, w_down):
    vm = pl.BlockSpec(memory_space=pltpu.VMEM)
    hbm = pl.BlockSpec(memory_space=pl.ANY)
    dma = pltpu.SemaphoreType.DMA
    flops = 9 * 2 * ROWS * D * FF
    lo, gt, gp, gg, gu, gd = pl.pallas_call(
        kernel,
        out_shape=(
            jax.ShapeDtypeStruct((TOK, D), BF16),
            jax.ShapeDtypeStruct((TOK, D), BF16),
            jax.ShapeDtypeStruct((TOP, TOK), F32),
            jax.ShapeDtypeStruct((D, FF), BF16),
            jax.ShapeDtypeStruct((D, FF), BF16),
            jax.ShapeDtypeStruct((FF, D), BF16),
        ),
        in_specs=[hbm, vm, vm, hbm, hbm, hbm, hbm],
        out_specs=(hbm, hbm, vm, hbm, hbm, hbm),
        scratch_shapes=[
            pltpu.VMEM((SA_ROWS, CW), BF16),
            pltpu.VMEM((NC, 2, NY, SR, CW), BF16),
            pltpu.VMEM((2, CW, FF), BF16),
            pltpu.VMEM((2, CW, FF), BF16),
            pltpu.VMEM((2, FF, CW), BF16),
            pltpu.VMEM((ROWS, FF), F32),
            pltpu.VMEM((ROWS, FF), F32),
            pltpu.VMEM((ROWS, FF), F32),
            pltpu.VMEM((ROWS, FF), BF16),
            pltpu.VMEM((ROWS, FF), BF16),
            pltpu.VMEM((ROWS, FF), BF16),
            pltpu.VMEM((NL, 2, SR, CW), BF16),
            pltpu.VMEM((NL, 2, 2, SR, CW), BF16),
            pltpu.VMEM((NF, 2, TOK, CW), BF16),
            pltpu.VMEM((NF, 2, 2, TOK, CW), BF16),
            pltpu.VMEM((NX, FR, CW), BF16),
            pltpu.VMEM((2, ROWS, NY * TOK), BF16),
            pltpu.VMEM((2, ROWS, TOK), F32),
            pltpu.VMEM((ROWS, ROWS), BF16),
            pltpu.VMEM((NY, TOP, TOK), jnp.int32),
            pltpu.VMEM((NY, TOP, TOK), F32),
            pltpu.VMEM((4, 8, ROWS), F32),
            pltpu.VMEM((TOK, D), BF16),
            pltpu.VMEM((TOK, D), BF16),
            dma((3, 2)), dma((NX,)), dma((NX,)),
            dma((2, 3, NC)), dma((2, 3, NC)), dma((2, 3, NC)), dma((2, 3, NC)),
            dma((NX,)), dma((NX,)), dma((3, NC)), dma((2, NC)),
            dma((2, 3)), dma((2, 3)), dma((3,)), dma((3,)), dma((2,)),
        ],
        compiler_params=pltpu.CompilerParams(
            collective_id=0, has_side_effects=True, vmem_limit_bytes=int(63.5 * 2**20)
        ),
        cost_estimate=pl.CostEstimate(flops=flops, bytes_accessed=37 * 2**20, transcendentals=ROWS * FF),
    )(tokens, gate_probs.T, expert_ids.T, cotangent, w_gate[0], w_up[0], w_down[0])
    gp, lo, gt, gg, gu, gd = keep(gp, lo, gt, gg, gu, gd)
    return lo, gt, gp.T, gg[None], gu[None], gd[None]


def solution(mesh):
    rows = P(("dp", "expert"), None)
    wide = P("expert", None, "dp")
    tall = P("expert", "dp", None)
    return jax.shard_map(
        on_device,
        mesh=mesh,
        in_specs=(rows, rows, rows, rows, wide, wide, tall),
        out_specs=(rows, rows, rows, wide, wide, tall),
        check_vma=False,
    )
```

time: 199 us -> 194 us (0.975)
  local copies, waits for them, and re-layouts: 13.6 us -> 0 us
  Pallas kernels: 183 us -> 193 us
    unnamed x14 -> x0, local copies, waits for them, and re-layouts: 13.6 us -> none
    pallas_call x0 -> x1, Pallas kernels: none -> 11.1 us  [keep(): pl.pallas_call(keep_kernel, out_shape=tuple((jax.ShapeDtypeStruct(a.shape...]
where the time goes in v3:
time: 194 us; the launch traced here: 193 us
  Pallas kernels  193 us (99%)
    pallas_call x1, Pallas kernels, on_device(): pl.pallas_call(kernel, out_shape=(jax.ShapeDtypeStruct((TOK, D), BF16), j...  182 us
    pallas_call x1, Pallas kernels, keep(): pl.pallas_call(keep_kernel, out_shape=tuple((jax.ShapeDtypeStruct(a.shape...  11.1 us

profile of v3, /device:TPU:1, one launch (start us, length us, event | category | flops | bytes accessed | tf_op | source)
XLA Modules:
  0.0 193.4 jit_solution(2535570260127324634)
XLA Ops:
  0.6 181.5 %shard_map.118 = (bf16[128,3584]{1,0:T(8,128)(2,1)}, bf16[128,3584]{1,0:T(8,128)(2,1)}, f32[8,128]{1,0:T(8,128)}, bf16[3584,512]{1,0:T(8,128)(2,1)}, bf16[3584,5...) custom-call(bf16[128,3584]{1,0:T(8,128)(2,1)} %tok_hbm.1, f32[8,128]{1,0:T(8,128)} %bitcast.15, s32[8,128]{1,0:T(8,128)} %bitcast.16, ...), custom_call_target="tpu_custom_call" | custom-call | flops 25367150592 | bytes 38797312 | tf_op jit(solution)/shard_map/pallas_call | solution.py:747
  182.2 11.1 %shard_map.119 = (f32[8,128]{1,0:T(8,128)}, bf16[128,3584]{1,0:T(8,128)(2,1)}, bf16[128,3584]{1,0:T(8,128)(2,1)}, bf16[3584,512]{1,0:T(8,128)(2,1)}, bf16[3584,5...) custom-call(f32[8,128]{1,0:T(8,128)} %get-tuple-element.18.refs_0_, bf16[128,3584]{1,0:T(8,128)(2,1)} %get-tuple-element.19.refs_1_, ...), custom_call_target="tpu_custom_call" | custom-call | tf_op jit(solution)/shard_map/pallas_call | solution.py:732

commit v4 on v3

--- a/solution.py
+++ b/solution.py
@@ -30,9 +30,7 @@
 TR = 2 * NY * TOK
 AF = NX * FR
 TB = 2 * NX * FR
-ST = TB + NX * TR
-SA_ROWS = ST + 3 * CW
-LARGE, PIECES = 5, 4
+SA_ROWS = TB + NX * TR
 PB = NF * FR
 STAGE = PB + NL * FR
 
@@ -65,21 +63,43 @@
 
 
 def kernel(
-    tok_hbm, probs, ids, cot_hbm, wg_hbm, wu_hbm, wd_hbm,
-    lo_hbm, gt_hbm, gp_out, gg_hbm, gu_hbm, gd_hbm,
-    sa, gath, wg, wu, wd, accg, accu, acch, hid, ggi, gui,
+    tok_hbm, probs_hbm, ids_hbm, cot_hbm, wg_hbm, wu_hbm, wd_hbm,
+    res, gp_out, gath,
+    sa, wg, wu, wd, accg, accu, acch, hid, ggi, gui,
     relay, vrec, relayf, vrecf, backf,
-    sel, pf, perm, idy, pry, zbuf, tok, cot,
-    wsem, asend, arecv, ysend, yrecv, rsend, rrecv, bsend, brecv, gsem, osem, tsend, trecv, zsend, zrecv, isem,
+    sel, pf, perm, idy, pry, zbuf, probs, ids,
+    wsem, asend, arecv, ysend, yrecv, rsend, rrecv, bsend, brecv, tsend, trecv, zsend, zrecv, isem, tabsem,
 ):
-    inputs = (
-        pltpu.make_async_copy(tok_hbm, tok, isem.at[0]),
-        pltpu.make_async_copy(cot_hbm, cot, isem.at[1]),
-    )
-    for c in inputs:
-        c.start()
     y = lax.axis_index("dp")
     e = lax.axis_index("expert")
+
+    def trow(q, kind, g):
+        return pl.ds(mo(TB + q * TR + kind * (NY * TOK) + g * TOK, TOK), TOK)
+
+    def input_copies(c):
+        q, g = jnp.minimum(c, NF), jnp.where(c < NF, y, c - NF)
+        return (
+            pltpu.make_async_copy(tok_hbm.at[:, columns(c)], sa.at[trow(q, 0, g)], isem.at[0, c]),
+            pltpu.make_async_copy(cot_hbm.at[:, columns(c)], sa.at[trow(q, 1, g)], isem.at[1, c]),
+        )
+
+    def start_inputs(c, carry):
+        for v in input_copies(c):
+            v.start()
+        return carry
+
+    def wait_inputs(c, carry):
+        for v in input_copies(c):
+            v.wait()
+        return carry
+
+    lax.fori_loop(0, NC, start_inputs, 0)
+    tables = (
+        pltpu.make_async_copy(probs_hbm, probs, tabsem.at[0]),
+        pltpu.make_async_copy(ids_hbm, ids, tabsem.at[1]),
+    )
+    for v in tables:
+        v.start()
     right, left, across = lax.rem(y + 1, NY), lax.rem(y + 3, NY), lax.rem(y + 2, NY)
     sides = (right, left)
     ex, ez, ec = e // 8, lax.rem(e // 2, 4), lax.rem(e, 2)
@@ -120,12 +140,9 @@
     load_weights(0)
     load_weights(1)
 
-    def trow(q, kind, g):
-        return pl.ds(mo(TB + q * TR + kind * (NY * TOK) + g * TOK, TOK), TOK)
-
     def first_copy(n, kind, d):
         return pltpu.make_async_remote_copy(
-            (tok, cot)[kind].at[:, columns(n)], sa.at[trow(n, kind, y)],
+            sa.at[trow(n, kind, y)], sa.at[trow(n, kind, y)],
             ysend.at[d, kind, n], yrecv.at[d, kind, n], device_id=(sides[d], e), device_id_type=MESH,
         )
 
@@ -151,8 +168,9 @@
                 first_copy(n, kind, d).start()
         return carry
 
-    for c in inputs:
-        c.wait()
+    lax.fori_loop(0, NC, wait_inputs, 0)
+    for v in tables:
+        v.wait()
     pl.semaphore_wait(barrier, NE + 2)
     lax.fori_loop(0, NF, start_first, 0)
     for c in table_copies():
@@ -189,13 +207,6 @@
 
     own_table = routing(ids[...], probs[...])
 
-    def stack(c, carry):
-        q, g = jnp.minimum(c, NF), jnp.where(c < NF, y, c - NF)
-        sa[trow(q, 0, g), :] = tok[:, columns(c)]
-        sa[trow(q, 1, g), :] = cot[:, columns(c)]
-        return carry
-
-    lax.fori_loop(NF, NC, stack, 0)
     place(1, [own_table] * NL)
 
     def plane_send(base, arrival, send_sem, recv_sem):
@@ -232,7 +243,6 @@
         plane_send(base, sa.at[mine], asend.at[q], arecv.at[q])
 
     build(NF, 1)
-    lax.fori_loop(0, NF, stack, 0)
 
     r_i = lax.broadcasted_iota(jnp.int32, (ROWS, TOK), 0)
     q_i = lax.broadcasted_iota(jnp.int32, (ROWS, TOK), 1)
@@ -246,14 +256,20 @@
     accu[...] = jnp.zeros((ROWS, FF), F32)
     acch[...] = jnp.zeros((ROWS, FF), F32)
 
+    def grow(c, kind, b):
+        return pl.ds(mo(c * (2 * ROWS) + kind * ROWS + b * SR, BLK), SR)
+
+    def gpair(c, kind, h):
+        return pl.ds(mo(c * (2 * ROWS) + kind * ROWS + h * 2 * SR, BLK), 2 * SR)
+
     def own_copy(c, kind, d):
-        ref = gath.at[c, kind, y]
+        ref = gath.at[grow(c, kind, y)]
         return pltpu.make_async_remote_copy(
             ref, ref, ysend.at[d, kind, c], yrecv.at[d, kind, c], device_id=(sides[d], e), device_id_type=MESH,
         )
 
     def pass_copy(c, d):
-        ref = gath.at[c, d, (left, right)[d]]
+        ref = gath.at[grow(c, d, (left, right)[d])]
         return pltpu.make_async_remote_copy(
             ref, ref, ysend.at[d, 2, c], yrecv.at[d, 2, c], device_id=(sides[d], e), device_id_type=MESH,
         )
@@ -289,11 +305,11 @@
             for h in range(2):
                 p = perm[h * 2 * SR : (h + 1) * 2 * SR, :]
                 rows = nn(p[:, : 2 * SR], pieces[0]) + nn(p[:, 2 * SR :], pieces[1])
-                store(kind, h, rows.astype(BF16).reshape(2, SR, CW))
+                store(kind, h, rows.astype(BF16))
 
     def keep_plane(kind, h, rows):
         for i in range(2):
-            gath[NF + 2 * h + i, kind, y] = rows[i]
+            gath[grow(NF + 2 * h + i, kind, y), :] = rows[i * SR : (i + 1) * SR]
 
     arrived(NF, keep_plane)
     for c in range(NF, NC):
@@ -325,7 +341,7 @@
         @pl.when(u < 2)
         def _():
             def keep_first(kind, h, rows):
-                gath[c, kind, 2 * h : 2 * h + 2] = rows
+                gath[gpair(c, kind, h), :] = rows
 
             arrived(c, keep_first)
 
@@ -340,8 +356,8 @@
 
         def half(h, carry2):
             rows = pl.ds(mo(h * 2 * SR, 2 * SR), 2 * SR)
-            xr = gath[c, 0, pl.ds(2 * h, 2)].reshape(2 * SR, CW)
-            cr = gath[c, 1, pl.ds(2 * h, 2)].reshape(2 * SR, CW)
+            xr = gath[gpair(c, 0, h), :]
+            cr = gath[gpair(c, 1, h), :]
             accg[rows, :] += nn(xr, wg[b])
             accu[rows, :] += nn(xr, wu[b])
             acch[rows, :] += nt(cr, wd[b])
@@ -357,7 +373,7 @@
     lax.fori_loop(0, NC - 1, gather_step, 0)
 
     def keep_last_first(kind, h, rows):
-        gath[NF - 1, kind, 2 * h : 2 * h + 2] = rows
+        gath[gpair(NF - 1, kind, h), :] = rows
 
     arrived(NF - 1, keep_last_first)
     for u in (NC - 1, NC):
@@ -411,7 +427,7 @@
     def middle(step, carry):
         b = lax.rem(y + jnp.where(step == 0, 2, jnp.where(step == 2, 3, jnp.where(step == 3, 0, 1))), NY)
         rows = pl.ds(mo(b * SR, SR), SR)
-        xr, cr = gath[NF - 1, 0, b], gath[NF - 1, 1, b]
+        xr, cr = gath[grow(NF - 1, 0, b), :], gath[grow(NF - 1, 1, b), :]
         accg[rows, :] += nn(xr, wg[now])
         accu[rows, :] += nn(xr, wu[now])
         acch[rows, :] += nt(cr, wd[now])
@@ -558,16 +574,14 @@
         for d in range(2):
             final_first(n, 1 - d, d).start()
 
-    def staged(m, k):
-        return pl.ds(mo(jnp.where(lax.rem(m, 2) == 0, ST + k * CW, TB + k * TR), CW), CW)
-
-    def grad_copies(m):
-        cols = columns(m)
-        return (
-            pltpu.make_async_copy(sa.at[staged(m, 0)], gg_hbm.at[cols], gsem.at[0, m]),
-            pltpu.make_async_copy(sa.at[staged(m, 1)], gu_hbm.at[cols], gsem.at[1, m]),
-            pltpu.make_async_copy(sa.at[staged(m, 2)], gd_hbm.at[:, cols], gsem.at[2, m]),
-        )
+    def drain_gathered(c, carry):
+        for d in range(2):
+            for kind in range(2):
+                own_copy(c, kind, d).wait_send()
+            pass_copy(c, d).wait_send()
+        return carry
+
+    lax.fori_loop(NF, NC, drain_gathered, 0)
 
     def scatter_step(i, carry):
         @pl.when((lax.rem(i, 2) == 1) & (i < 6))
@@ -592,17 +606,12 @@
             parts_sent(0)
             send_back(NF, PB)
 
-        @pl.when(i >= 2)
-        def _():
-            for c in grad_copies(i - 2):
-                c.wait()
-
-        xr = gath[i, 0].reshape(ROWS, CW)
-        sa[staged(i, 0), :] = tn(xr, ggi[...]).astype(BF16)
-        sa[staged(i, 1), :] = tn(xr, gui[...]).astype(BF16)
-        sa[staged(i, 2), :] = tn(hid[...], gath[i, 1].reshape(ROWS, CW)).astype(BF16)
-        for c in grad_copies(i):
-            c.start()
+        base = i * (2 * ROWS)
+        xr = gath[pl.ds(mo(base, BLK), ROWS), :]
+        cr = gath[pl.ds(mo(base + ROWS, BLK), ROWS), :]
+        grads = [tn(xr, ggi[...]).astype(BF16), tn(xr, gui[...]).astype(BF16), tn(hid[...], cr).astype(BF16)]
+        for k, v in enumerate(grads):
+            gath[pl.ds(mo(base + k * CW, BLK), CW), :] = v
         return carry
 
     lax.fori_loop(0, NC, scatter_step, 0)
@@ -622,14 +631,6 @@
     for c in score_copies():
         c.start()
 
-    def result_copy(n, kind):
-        out = (lo_hbm, gt_hbm)[kind].at[:, columns(n)]
-        return pltpu.make_async_copy(backf.at[n, pl.ds(kind * TOK, TOK)], out, osem.at[kind, n])
-
-    def last_copy(l, kind):
-        rows = pl.ds(mo(STAGE + kind * (NY * TOK) + l * TOK, TOK), TOK)
-        return pltpu.make_async_copy(sa.at[rows], (lo_hbm, gt_hbm)[kind].at[:, columns(NF + l)], osem.at[kind, NF + l])
-
     def last_first(n, carry):
         for d in range(2):
             for kind in range(2):
@@ -637,16 +638,14 @@
         for kind in range(2):
             own = sa[fpart(n, kind, y), :].astype(F32)
             total = own + vrecf[n, 0, kind].astype(F32) + vrecf[n, 1, kind].astype(F32)
-            backf[n, kind * TOK : (kind + 1) * TOK, :] = total.astype(BF16)
-            result_copy(n, kind).start()
+            res[kind, n] = total.astype(BF16)
         return carry
 
     lax.fori_loop(0, NF, last_first, 0)
 
     def keep_last(kind, v):
-        sa[pl.ds(STAGE + kind * NY * TOK, NY * TOK), :] = v.astype(BF16)
         for l in range(NL):
-            last_copy(l, kind).start()
+            res[kind, NF + l] = v[l * TOK : (l + 1) * TOK].astype(BF16)
 
     sum_tokens(NF, 1, keep_last)
 
@@ -667,22 +666,11 @@
     for k in range(TOP):
         gp_out[k : k + 1, :] = jnp.sum(jnp.where(ids[k : k + 1, :] == esub, score, 0.0), axis=0, keepdims=True)
 
-    def drain(c, carry):
-        l = c - NF
-        for d in range(2):
-            for kind in range(2):
-                own_copy(c, kind, d).wait_send()
-            pass_copy(c, d).wait_send()
-        for kind in range(2):
-            last_copy(l, kind).wait()
-
-        @pl.when(l >= 1)
-        def _():
-            parts_sent(l)
-
-        return carry
-
-    lax.fori_loop(NF, NC, drain, 0)
+    def drain(l, carry):
+        parts_sent(l)
+        return carry
+
+    lax.fori_loop(1, NL, drain, 0)
     wait_plane(bsend.at[NF])
 
     def drain_first(n, carry):
@@ -690,62 +678,34 @@
             for kind in range(2):
                 final_first(n, kind, d).wait_send()
             relay_first(n, d).wait_send()
-        for kind in range(2):
-            result_copy(n, kind).wait()
         return carry
 
     lax.fori_loop(0, NF, drain_first, 0)
     for c in table_copies() + score_copies():
         c.wait_send()
-    for m in range(NC - 2, NC):
-        for c in grad_copies(m):
-            c.wait()
-
-
-def keep_kernel(*refs):
-    small, small_out = refs[0], refs[LARGE + 1]
-    small_out[...] = small[...]
-    refs = refs[1 : LARGE + 1] + refs[LARGE + 2 :]
-    count = LARGE
-    rsem, wsem = refs[-2:]
-    reads, writes = [], []
-    for k in range(PIECES):
-        for i in range(count):
-            src, dst, held = refs[i], refs[count + i], refs[2 * count + i]
-            step = src.shape[0] // PIECES
-            rows = pl.ds(k * step, step)
-            reads.append(pltpu.make_async_copy(src.at[rows], held.at[rows], rsem.at[i, k]))
-            writes.append(pltpu.make_async_copy(held.at[rows], dst.at[rows], wsem.at[i, k]))
-    for c in reads:
+
+def keep_kernel(res, gp, grads, lo_out, gt_out, gp_out, gg_out, gu_out, gd_out, sem):
+    gp_out[...] = gp[...]
+    copies = []
+    for c in range(NC):
+        cols = pl.ds(c * CW, CW)
+        pairs = [
+            (grads.at[pl.ds((3 * c + k) * CW, CW)], out)
+            for k, out in enumerate((gg_out.at[cols], gu_out.at[cols], gd_out.at[:, cols]))
+        ]
+        pairs += [(res.at[k, c], out.at[:, cols]) for k, out in enumerate((lo_out, gt_out))]
+        copies += [pltpu.make_async_copy(src, dst, sem.at[k, c]) for k, (src, dst) in enumerate(pairs)]
+    for c in copies:
         c.start()
-    for r, w in zip(reads, writes):
-        r.wait()
-        w.start()
-    for w in writes:
-        w.wait()
-
-
-def keep(small, *arrays):
+    for c in copies:
+        c.wait()
+
+
+def keep(res, gp, grads):
     vm = pl.BlockSpec(memory_space=pltpu.VMEM)
     hbm = pl.BlockSpec(memory_space=pl.ANY)
-    sems = pltpu.SemaphoreType.DMA((LARGE, PIECES))
     return pl.pallas_call(
         keep_kernel,
-        out_shape=tuple(jax.ShapeDtypeStruct(a.shape, a.dtype) for a in (small, *arrays)),
-        in_specs=[vm] + [hbm] * LARGE,
-        out_specs=(vm,) + (hbm,) * LARGE,
-        scratch_shapes=[pltpu.VMEM(a.shape, a.dtype) for a in arrays] + [sems, sems],
-        compiler_params=pltpu.CompilerParams(vmem_limit_bytes=63 * 2**20),
-    )(small, *arrays)
-
-
-def on_device(tokens, gate_probs, expert_ids, cotangent, w_gate, w_up, w_down):
-    vm = pl.BlockSpec(memory_space=pltpu.VMEM)
-    hbm = pl.BlockSpec(memory_space=pl.ANY)
-    dma = pltpu.SemaphoreType.DMA
-    flops = 9 * 2 * ROWS * D * FF
-    lo, gt, gp, gg, gu, gd = pl.pallas_call(
-        kernel,
         out_shape=(
             jax.ShapeDtypeStruct((TOK, D), BF16),
             jax.ShapeDtypeStruct((TOK, D), BF16),
@@ -754,11 +714,29 @@
             jax.ShapeDtypeStruct((D, FF), BF16),
             jax.ShapeDtypeStruct((FF, D), BF16),
         ),
-        in_specs=[hbm, vm, vm, hbm, hbm, hbm, hbm],
+        in_specs=[hbm, vm, hbm],
         out_specs=(hbm, hbm, vm, hbm, hbm, hbm),
+        scratch_shapes=[pltpu.SemaphoreType.DMA((5, NC))],
+        compiler_params=pltpu.CompilerParams(vmem_limit_bytes=8 * 2**20),
+    )(res, gp, grads)
+
+
+def on_device(tokens, gate_probs, expert_ids, cotangent, w_gate, w_up, w_down):
+    vm = pl.BlockSpec(memory_space=pltpu.VMEM)
+    hbm = pl.BlockSpec(memory_space=pl.ANY)
+    dma = pltpu.SemaphoreType.DMA
+    flops = 9 * 2 * ROWS * D * FF
+    res, gp, grads = pl.pallas_call(
+        kernel,
+        out_shape=(
+            pltpu.VMEM((2, NC, TOK, CW), BF16),
+            pltpu.VMEM((TOP, TOK), F32),
+            pltpu.VMEM((NC * 2 * ROWS, CW), BF16),
+        ),
+        in_specs=[hbm] * 7,
+        out_specs=(vm, vm, vm),
         scratch_shapes=[
             pltpu.VMEM((SA_ROWS, CW), BF16),
-            pltpu.VMEM((NC, 2, NY, SR, CW), BF16),
             pltpu.VMEM((2, CW, FF), BF16),
             pltpu.VMEM((2, CW, FF), BF16),
             pltpu.VMEM((2, FF, CW), BF16),
@@ -779,19 +757,19 @@
             pltpu.VMEM((NY, TOP, TOK), jnp.int32),
             pltpu.VMEM((NY, TOP, TOK), F32),
             pltpu.VMEM((4, 8, ROWS), F32),
-            pltpu.VMEM((TOK, D), BF16),
-            pltpu.VMEM((TOK, D), BF16),
+            pltpu.VMEM((TOP, TOK), F32),
+            pltpu.VMEM((TOP, TOK), jnp.int32),
             dma((3, 2)), dma((NX,)), dma((NX,)),
             dma((2, 3, NC)), dma((2, 3, NC)), dma((2, 3, NC)), dma((2, 3, NC)),
-            dma((NX,)), dma((NX,)), dma((3, NC)), dma((2, NC)),
-            dma((2, 3)), dma((2, 3)), dma((3,)), dma((3,)), dma((2,)),
+            dma((NX,)), dma((NX,)),
+            dma((2, 3)), dma((2, 3)), dma((3,)), dma((3,)), dma((2, NC)), dma((2,)),
         ],
         compiler_params=pltpu.CompilerParams(
-            collective_id=0, has_side_effects=True, vmem_limit_bytes=int(63.5 * 2**20)
+            collective_id=0, has_side_effects=True, vmem_limit_bytes=int(51.25 * 2**20)
         ),
         cost_estimate=pl.CostEstimate(flops=flops, bytes_accessed=37 * 2**20, transcendentals=ROWS * FF),
     )(tokens, gate_probs.T, expert_ids.T, cotangent, w_gate[0], w_up[0], w_down[0])
-    gp, lo, gt, gg, gu, gd = keep(gp, lo, gt, gg, gu, gd)
+    lo, gt, gp, gg, gu, gd = keep(res, gp, grads)
     return lo, gt, gp.T, gg[None], gu[None], gd[None]
 
 

time: 194 us -> 187 us (0.964)
  Pallas kernels: 193 us -> 186 us
    pallas_call x2, Pallas kernels: 193 us -> 186 us  [the longest x1 181 us: on_device(): pl.pallas_call(kernel, out_shape=(pltpu.VMEM((2, NC, TOK, CW), BF16), plt...]
where the time goes in v4:
time: 187 us
  Pallas kernels  186 us (99%)
    pallas_call x1, Pallas kernels, on_device(): pl.pallas_call(kernel, out_shape=(pltpu.VMEM((2, NC, TOK, CW), BF16), plt...  181 us
    pallas_call x1, Pallas kernels, keep(): pl.pallas_call(keep_kernel, out_shape=(jax.ShapeDtypeStruct((TOK, D), BF1...  5.49 us

profile of v4, /device:TPU:1, one launch (start us, length us, event | category | flops | bytes accessed | tf_op | source)
XLA Modules:
  0.0 187.0 jit_solution(1917262722396494020)
XLA Ops:
  0.6 180.7 %shard_map.118 = (bf16[2,7,128,512]{3,2,1,0:T(8,128)(2,1)S(1)}, f32[8,128]{1,0:T(8,128)S(1)}, bf16[10752,512]{1,0:T(8,128)(2,1)S(1)}) custom-call(bf16[128,3584]{1,0:T(8,128)(2,1)} %tok_hbm.1, f32[8,128]{1,0:T(8,128)} %bitcast.15, s32[8,128]{1,0:T(8,128)} %bitcast.16, bf16[128,3584]{1,0:T(8,128)(2,1)} %cot_hbm.1, bf16[3584,512]{1,0:T(8,128)(2,1)} %bitcast.9, ...), custom_call_target="tpu_custom_call" | custom-call | flops 25367150592 | bytes 38797312 | tf_op jit(solution)/shard_map/pallas_call | solution.py:729
  181.4 5.5 %shard_map.119 = (bf16[128,3584]{1,0:T(8,128)(2,1)}, bf16[128,3584]{1,0:T(8,128)(2,1)}, f32[8,128]{1,0:T(8,128)}, bf16[3584,512]{1,0:T(8,128)(2,1)}, bf16[3584,5...) custom-call(bf16[2,7,128,512]{3,2,1,0:T(8,128)(2,1)S(1)} %get-tuple-element.15.res, f32[8,128]{1,0:T(8,128)S(1)} %get-tuple-element.16.gp, ...), custom_call_target="tpu_custom_call" | custom-call | tf_op jit(solution)/shard_map/pallas_call | solution.py:707

commit v5 on v4

--- a/solution.py
+++ b/solution.py
@@ -551,7 +551,7 @@
             return halves(backf[q, h * (FR // 2) : (h + 1) * (FR // 2), :], NE // 2)[kind]
 
         for h, rows in enumerate(parts):
-            prod = nn(sel[k, rows, :], tc) * rows_of(h, 0)
+            prod = (accu[rows, :] if k else nn(sel[k, rows, :], tc)) * rows_of(h, 0)
             z = prod[:, :TOK]
             for b in range(1, CW // TOK):
                 z = z + prod[:, b * TOK : (b + 1) * TOK]
@@ -631,6 +631,10 @@
     for c in score_copies():
         c.start()
 
+    for h in range(2):
+        last_c = sa[pl.ds(mo(TB + NF * TR + NY * TOK, TOK), NY * TOK), :]
+        accu[h * 2 * SR : (h + 1) * 2 * SR, :] = nn(sel[1, h * 2 * SR : (h + 1) * 2 * SR, :], last_c)
+
     def last_first(n, carry):
         for d in range(2):
             for kind in range(2):
@@ -642,12 +646,6 @@
         return carry
 
     lax.fori_loop(0, NF, last_first, 0)
-
-    def keep_last(kind, v):
-        for l in range(NL):
-            res[kind, NF + l] = v[l * TOK : (l + 1) * TOK].astype(BF16)
-
-    sum_tokens(NF, 1, keep_last)
 
     for c in score_copies():
         c.wait_recv()
@@ -657,6 +655,13 @@
     z0, z1, z2 = split3(jnp.where(group, jnp.broadcast_to(zrow[0:1], (NE, ROWS)), 0.0))
     mine = sel[0, :, pl.ds(mo(y * TOK, TOK), TOK)]
     score = nn(z0, mine) + nn(z1, mine) + nn(z2, mine)
+
+    def keep_last(kind, v):
+        for l in range(NL):
+            res[kind, NF + l] = v[l * TOK : (l + 1) * TOK].astype(BF16)
+
+    sum_tokens(NF, 1, keep_last)
+
     z0, z1, z2 = split3(accg[:, TOK : 2 * TOK])
     zrow = nt(ones, z0) + nt(ones, z1) + nt(ones, z2)
     z0, z1, z2 = split3(jnp.where(group, jnp.broadcast_to(zrow[0:1], (NE, ROWS)), 0.0))

time: 187 us -> 187 us (level)
  no operation moved by 1% of the time
where the time goes in v5:
time: 187 us; the launch traced here: 186 us
  Pallas kernels  186 us (99%)
    pallas_call x1, Pallas kernels, on_device(): pl.pallas_call(kernel, out_shape=(pltpu.VMEM((2, NC, TOK, CW), BF16), plt...  180 us
    pallas_call x1, Pallas kernels, keep(): pl.pallas_call(keep_kernel, out_shape=(jax.ShapeDtypeStruct((TOK, D), BF1...  5.49 us

profile of v5, /device:TPU:1, one launch (start us, length us, event | category | flops | bytes accessed | tf_op | source)
XLA Modules:
  0.0 186.4 jit_solution(12377111483054530869)
XLA Ops:
  0.6 180.1 %shard_map.118 = (bf16[2,7,128,512]{3,2,1,0:T(8,128)(2,1)S(1)}, f32[8,128]{1,0:T(8,128)S(1)}, bf16[10752,512]{1,0:T(8,128)(2,1)S(1)}) custom-call(bf16[128,3584]{1,0:T(8,128)(2,1)} %tok_hbm.1, f32[8,128]{1,0:T(8,128)} %bitcast.15, s32[8,128]{1,0:T(8,128)} %bitcast.16, bf16[128,3584]{1,0:T(8,128)(2,1)} %cot_hbm.1, bf16[3584,512]{1,0:T(8,128)(2,1)} %bitcast.9, ...), custom_call_target="tpu_custom_call" | custom-call | flops 25367150592 | bytes 38797312 | tf_op jit(solution)/shard_map/pallas_call | solution.py:734
  180.7 5.5 %shard_map.119 = (bf16[128,3584]{1,0:T(8,128)(2,1)}, bf16[128,3584]{1,0:T(8,128)(2,1)}, f32[8,128]{1,0:T(8,128)}, bf16[3584,512]{1,0:T(8,128)(2,1)}, bf16[3584,5...) custom-call(bf16[2,7,128,512]{3,2,1,0:T(8,128)(2,1)S(1)} %get-tuple-element.15.res, f32[8,128]{1,0:T(8,128)S(1)} %get-tuple-element.16.gp, ...), custom_call_target="tpu_custom_call" | custom-call | tf_op jit(solution)/shard_map/pallas_call | solution.py:712
